TPU v7x, 128 devices: a whole 4x4x4 slice. The times are simulated.
128 devices in a mesh: freq: 4 (over x), tile: 32 (over z, y, core).
Axes of the slice: x: 4, y: 4, z: 4, core: 2. Of those that a mesh axis runs over, the one named last changes fastest.
Arguments:
- x_time: float32 [8192, 64, 256], P(('tile', 'freq')), may hold values from -4 to 4
- mute: int32 [8192], P(('tile', 'freq')), may hold values from 0 to 175, as said below
- ranks: int32 [4, 32, 32], P('freq'), may hold values from 8 to 64, as said below
- right_factor_columns: float32 [4, 2, 32, 256, 2048], P('freq', None, 'tile'), may hold values from -0.375 to 0.375
- u_rows: float32 [4, 2, 32, 256, 2048], P('freq', None, 'tile'), may hold values from -0.1875 to 0.1875
- data: float32 [4, 2, 8192, 64], P('freq', None, 'tile'), may hold values from -6 to 6
Outputs:
- x_out: float32 [8192, 64, 256], P(('tile', 'freq'))
- resid: float32 [4, 2, 8192, 64], P('freq', None, 'tile')
Inputs may be any that keep to these rules, and one draw needn't show every extreme that they name: mute never falls with the receiver index. `ranks`: at each frequency, the 1 tile rows of some index of tile have rank 64 in every tile column.
All inputs are finite; a program needn't handle non-finite values.
Results may differ from a plain program's by a relative error of at most 0.0003.
Values sent between devices are 32-bit elements; how exact they have to be, the bound alone decides.
A program may use at most 192 MiB of HBM per device.

v0:
```python
import jax
import jax.numpy as jnp
from jax import lax
from jax.sharding import PartitionSpec as P

FLO = 16
ITERS = 2


HIGH = lax.Precision.HIGHEST


def mat_mul(left, right):
    return jnp.dot(left, right, precision=HIGH, preferred_element_type=jnp.float32)


def mat_tmul(left, right):
    return lax.dot_general(
        left, right, (((0,), (0,)), ((), ())), precision=HIGH, preferred_element_type=jnp.float32
    )


def conjugate_product(matrix, model_wavefield):
    real = mat_tmul(matrix[0], model_wavefield[0]) + mat_tmul(matrix[1], model_wavefield[1])
    imag = mat_tmul(matrix[0], model_wavefield[1]) - mat_tmul(matrix[1], model_wavefield[0])
    return jnp.stack([real, imag])


def direct_product(matrix, model_wavefield):
    real = mat_mul(matrix[0], model_wavefield[0]) - mat_mul(matrix[1], model_wavefield[1])
    imag = mat_mul(matrix[0], model_wavefield[1]) + mat_mul(matrix[1], model_wavefield[0])
    return jnp.stack([real, imag])


def body(x_time, mute, ranks, right_factor_columns, u_rows, data):
    nfreq = lax.axis_size("freq")
    ntile = lax.axis_size("tile")
    tidx = lax.axis_index("tile")
    block = x_time.shape[0]
    samples = x_time.shape[2]
    rcol = right_factor_columns.shape[4]
    rrow = u_rows.shape[4]
    rows_here = u_rows.shape[2]
    rank_f = ranks[0]
    ntr = rank_f.shape[0]
    kmax = rcol // ntr
    col_off = jnp.cumsum(rank_f, axis=0) - rank_f
    row_off = jnp.cumsum(rank_f, axis=1) - rank_f
    right_factor_matrix = right_factor_columns[0, :, 0]
    umat = u_rows[0]
    ranks_col = rank_f[:, tidx]
    offs_col = col_off[:, tidx]
    inner_k = jnp.arange(kmax, dtype=jnp.int32)
    steps = jnp.arange(samples, dtype=jnp.int32)
    freqs = FLO + jnp.arange(nfreq, dtype=jnp.int32)
    angle = (freqs[:, None] * steps[None, :] % samples).astype(jnp.float32) * (
        2.0 * jnp.pi / samples
    )
    cosines = jnp.cos(angle)
    sines = jnp.sin(angle)
    keep = (steps[None, :] >= mute[:, None]).astype(jnp.float32)

    def spectra(model_wavefield):
        real = jnp.einsum(
            "rvt,ft->frv",
            model_wavefield,
            cosines,
            precision=HIGH,
            preferred_element_type=jnp.float32,
        )
        imag = -jnp.einsum(
            "rvt,ft->frv",
            model_wavefield,
            sines,
            precision=HIGH,
            preferred_element_type=jnp.float32,
        )
        spec = jnp.stack([real, imag], axis=1)
        return lax.all_to_all(spec, "freq", split_axis=0, concat_axis=2, tiled=True)[0]

    def apply_here(model_wavefield):
        column_contributions = conjugate_product(right_factor_matrix, model_wavefield)
        seg_rank = ranks_col.reshape(ntile, rows_here)
        seg_off = offs_col.reshape(ntile, rows_here)
        valid = inner_k[None, None, :] < seg_rank[:, :, None]
        source = jnp.where(valid, seg_off[:, :, None] + inner_k[None, None, :], 0)
        packed = jnp.where(valid[None, :, :, :, None], column_contributions[:, source], 0.0)
        arrived = lax.all_to_all(packed, "tile", split_axis=1, concat_axis=1, tiled=True)
        slots = jnp.arange(rrow, dtype=jnp.int32)
        row = tidx * rows_here + 0
        offsets = row_off[row]
        which = jnp.sum((offsets[None, :] <= slots[:, None]).astype(jnp.int32), axis=1) - 1
        inner = slots - offsets[which]
        live = inner < rank_f[row][which]
        picked = arrived[:, which, 0, jnp.minimum(inner, kmax - 1)]
        collected_pieces = jnp.where(live[None, :, None], picked, 0.0)
        outputs = direct_product(umat[:, 0], collected_pieces)
        return outputs

    x_out = x_time
    resid = apply_here(spectra(x_time)) - data[0]
    for step in range(ITERS):
        width = umat.shape[2]
        pieces = resid.reshape(2, rows_here, width, resid.shape[2])
        row_terms = jnp.stack([conjugate_product(umat[:, 0], pieces[:, 0])], axis=1)
        mine = tidx * rows_here + jnp.arange(rows_here, dtype=jnp.int32)
        adjoint_seg_off = row_off[mine].T
        adjoint_seg_rank = rank_f[mine].T
        adjoint_valid = inner_k[None, None, :] < adjoint_seg_rank[:, :, None]
        adjoint_source = jnp.where(
            adjoint_valid, adjoint_seg_off[:, :, None] + inner_k[None, None, :], 0
        )
        local_ids = jnp.arange(rows_here, dtype=jnp.int32)[None, :, None]
        adjoint_packed = jnp.where(
            adjoint_valid[None, :, :, :, None], row_terms[:, local_ids, adjoint_source], 0.0
        )
        adjoint_arrived = lax.all_to_all(
            adjoint_packed, "tile", split_axis=1, concat_axis=1, tiled=True
        )
        flat = adjoint_arrived.reshape(2, ntr * kmax, adjoint_arrived.shape[4])
        adjoint_slots = jnp.arange(rcol, dtype=jnp.int32)
        adjoint_which = (
            jnp.sum((offs_col[None, :] <= adjoint_slots[:, None]).astype(jnp.int32), axis=1) - 1
        )
        adjoint_inner = adjoint_slots - offs_col[adjoint_which]
        adjoint_live = adjoint_inner < ranks_col[adjoint_which]
        adjoint_collected_pieces = jnp.where(
            adjoint_live[None, :, None],
            flat[:, adjoint_which * kmax + jnp.minimum(adjoint_inner, kmax - 1)],
            0.0,
        )
        adjoint_spec = direct_product(right_factor_matrix, adjoint_collected_pieces)
        parts = adjoint_spec.reshape(2, nfreq, block, adjoint_spec.shape[2])[None]
        arrived = lax.all_to_all(parts, "freq", split_axis=2, concat_axis=0, tiled=True)[:, :, 0]
        to_real = jnp.einsum(
            "frv,ft->rvt",
            arrived[:, 0],
            cosines,
            precision=HIGH,
            preferred_element_type=jnp.float32,
        )
        to_imag = jnp.einsum(
            "frv,ft->rvt", arrived[:, 1], sines, precision=HIGH, preferred_element_type=jnp.float32
        )
        grad = (to_real - to_imag) * keep[:, None, :]
        grad_spec = spectra(grad)
        grad_norm_local = jnp.sum(grad * grad)
        grad_norm = lax.psum(grad_norm_local, ("freq", "tile"))
        image = apply_here(grad_spec)
        image_norm_local = jnp.sum(image * image)
        image_norm = lax.psum(image_norm_local, ("freq", "tile"))
        alpha = grad_norm / image_norm
        x_out = x_out - alpha * grad
        resid = resid - alpha * image
    return (x_out, resid[None])


def solution(mesh):
    in_specs = (
        P(("tile", "freq"), None, None),
        P(("tile", "freq")),
        P("freq", None, None),
        P("freq", None, "tile", None, None),
        P("freq", None, "tile", None, None),
        P("freq", None, "tile", None),
    )
    out_specs = (P(("tile", "freq"), None, None), P("freq", None, "tile", None))
    return jax.shard_map(body, mesh=mesh, in_specs=in_specs, out_specs=out_specs, check_vma=False)
```

profile of v0, /device:TPU:1, one launch (start us, length us, event | category | flops | bytes accessed | tf_op | source)
XLA Modules:
  0.0 778.4 jit_solution(8474464808787118856)
XLA Ops:
  0.7 7.4 convolution_bitcast_fusion.2
  8.1 5.1 fusion.82
  14.1 5.2 all-to-all-start
  23.7 4.4 compare_select_fusion.19
  29.8 4.5 compare_select_fusion.18
  35.1 31.9 %select_compare_fusion.1 = (pred[2048]{0:T(1024)(128)(4,1)}, s32[2048]{0:T(1024)S(1)}) fusion(pred[2048]{0:T(1024)(128)(4,1)S(1)} %get-tuple-element.48, pred[2048]{0:T(1024)(128)(4,1)S(1)} %get-tuple-element.47, pred[2048]{0:T(1024)(128)(4,1)S(1)} %get-tuple-element.46, pred[2048]{0:T(1024)(128)(4,1)S(1)} %get-tuple-element.45, ...), kind=kLoop, calls=%fused_computation.350 | loop fusion | flops 106496 | bytes 78024 | tf_op jit(solution)/shard_map/lt | solution.py:126
  67.0 4.9 compare_select_fusion.7
  72.0 4.4 compare_select_fusion.6
  78.7 3.1 fusion.78
  88.8 14.6 %gather_fusion = f32[2048,2,64]{2,1,0:T(2,128)} fusion(f32[2,2048,64]{2,0,1:T(2,128)S(1)} %copy.50, s32[2048]{0:T(1024)S(1)} %broadcast_clamp_fusion.1), kind=kCustom, calls=%fused_computation | custom fusion | bytes 2105344 | tf_op jit(solution)/shard_map/gather | solution.py:87
  103.4 5.6 fusion.251
  109.0 3.2 reshape.1331
  112.2 21.7 %all-to-all-start.1 = ((f32[32,1,8192]{2,1,0:T(1,128)}), f32[32,1,8192]{2,1,0:T(1,128)S(1)}, u32[]{:S(2)}, u32[]{:S(2)}) async-start(f32[32,1,8192]{2,1,0:T(1,128)} %reshape.1331), calls=%async_computation.1 | async-start | bytes 2097152 | tf_op jit(solution)/shard_map/all_to_all | solution.py:88
  135.3 31.4 %select_compare_fusion = (pred[2048]{0:T(1024)(128)(4,1)S(1)}, s32[2048]{0:T(1024)S(1)}) fusion(pred[2048]{0:T(1024)(128)(4,1)S(1)} %get-tuple-element.73, pred[2048]{0:T(1024)(128)(4,1)S(1)} %get-tuple-element.72, pred[2048]{0:T(1024)(128)(4,1)S(1)} %get-tuple-element.71, pred[2048]{0:T(1024)(128)(4,1)S(1)} %get-tuple-element.70, ...), kind=kLoop, calls=%fused_computation.348 | loop fusion | flops 106496 | bytes 78024 | tf_op jit(solution)/shard_map/lt | solution.py:94
  166.7 3.2 reduce.105
  172.8 10.3 %gather_fusion.1 = f32[2048,2,64]{2,1,0:T(2,128)S(1)} fusion(f32[2,32,1,64,64]{4,0,3,2,1:T(2,128)} %bitcast.594, s32[2048]{0:T(1024)S(1)} %bitcast.564), kind=kCustom, calls=%fused_computation.1 | custom fusion | bytes 2121728 | tf_op jit(solution)/shard_map/gather | solution.py:95
  183.1 7.4 select_bitcast_fusion.4
  207.0 15.5 %gather_fusion.2 = f32[2048,2,64]{2,1,0:T(2,128)} fusion(f32[2,1,2048,64]{3,0,2,1:T(2,128)S(1)} %copy.51, s32[2048]{0:T(1024)S(1)} %reshape.770), kind=kCustom, calls=%fused_computation.2 | custom fusion | bytes 2113536 | tf_op jit(solution)/shard_map/gather | solution.py:115
  222.5 5.6 fusion.249
  228.1 3.2 reshape.1333
  231.3 7.4 all-to-all-start.2
  238.7 17.1 %all-to-all-done.2 = f32[32,1,8192]{2,1,0:T(1,128)S(1)} async-done(((f32[32,1,8192]{2,1,0:T(1,128)}), f32[32,1,8192]{2,1,0:T(1,128)S(1)}, u32[]{:S(2)}, u32[]{:S(2)}) %all-to-all-start.2) | async-done | bytes 1048608 | tf_op jit(solution)/shard_map/all_to_all | solution.py:117
  255.8 3.2 reduce.106
  261.9 8.4 %gather_fusion.3 = f32[2048,2,64]{2,1,0:T(2,128)S(1)} fusion(f32[2,2048,64]{2,0,1:T(2,128)} %bitcast.595, s32[2048]{0:T(1024)S(1)} %broadcast_clamp_fusion), kind=kCustom, calls=%fused_computation.3 | custom fusion | bytes 2105344 | tf_op jit(solution)/shard_map/gather | solution.py:129
  270.3 7.4 select_bitcast_fusion.1
  285.7 3.5 fusion.92
  290.1 4.7 all-to-all-start.3
  294.9 4.6 all-to-all-done.3
  300.8 3.6 fusion.166
  304.4 4.5 multiply_reduce_fusion.1
  308.9 5.1 convolution_bitcast_fusion.1
  314.0 5.3 fusion.81
  319.6 7.2 all_to_all.100
  328.0 3.1 fusion.70
  338.1 14.5 %gather_fusion.4 = f32[2048,2,64]{2,1,0:T(2,128)} fusion(f32[2,2048,64]{2,0,1:T(2,128)S(1)} %copy.58, s32[2048]{0:T(1024)S(1)} %copy-done.17), kind=kCustom, calls=%fused_computation.4 | custom fusion | bytes 2105344 | tf_op jit(solution)/shard_map/gather | solution.py:87
  352.6 5.6 fusion.252
  360.5 23.3 %all_to_all.101 = f32[32,1,8192]{2,1,0:T(1,128)S(1)} all-to-all(f32[32,1,8192]{2,1,0:T(1,128)S(1)} %reshape.1339), channel_id=1, replica_groups=mesh['freq'=4,'tile'=32] {'tile'}, dimensions={0} | all-to-all | bytes 2097152 | tf_op jit(solution)/shard_map/all_to_all | solution.py:88
  383.8 3.2 reduce.109
  388.5 17.6 %gather_fusion.5 = f32[2048,2,64]{2,1,0:T(2,128)} fusion(f32[2,32,1,64,64]{4,0,3,2,1:T(2,128)S(1)} %bitcast.596, s32[2048]{0:T(1024)S(1)} %bitcast.565), kind=kCustom, calls=%fused_computation.5 | custom fusion | bytes 2121728 | tf_op jit(solution)/shard_map/gather | solution.py:95
  406.1 10.0 %select_bitcast_fusion.3 = f32[2,2048,64]{2,0,1:T(2,128)S(1)} fusion(f32[2048,2,64]{2,1,0:T(2,128)} %gather_fusion.5, pred[2048]{0:T(1024)(128)(4,1)S(1)} %copy-done.30), kind=kLoop, calls=%fused_computation.108 | loop fusion | flops 262144 | bytes 2099200 | tf_op jit(solution)/shard_map/jit(_where)/select_n | solution.py:96
  426.4 63.1 %all-reduce.2 = (f32[]{:T(128)}, f32[]{:T(128)}) all-reduce(f32[]{:T(128)} %get-tuple-element.240, f32[]{:T(128)} %multiply_reduce_fusion.2), channel_id=1, replica_groups=mesh['freq'=4,'tile'=32] {'freq','tile'}, use_global_device_ids=true, to_apply=%region_5.6 | all-reduce | flops 2 | bytes 16 | tf_op jit(solution)/shard_map/psum | solution.py:148
  490.9 3.1 fusion.32
  500.9 15.1 %gather_fusion.6 = f32[2048,2,64]{2,1,0:T(2,128)} fusion(f32[2,1,2048,64]{3,0,2,1:T(2,128)S(1)} %copy.59, s32[2048]{0:T(1024)S(1)} %reshape.770), kind=kCustom, calls=%fused_computation.6 | custom fusion | bytes 2113536 | tf_op jit(solution)/shard_map/gather | solution.py:115
  516.0 5.6 fusion.250
  523.9 22.0 %all_to_all.102 = f32[32,1,8192]{2,1,0:T(1,128)S(1)} all-to-all(f32[32,1,8192]{2,1,0:T(1,128)S(1)} %reshape.1341), channel_id=1, replica_groups=mesh['freq'=4,'tile'=32] {'tile'}, dimensions={0} | all-to-all | bytes 2097152 | tf_op jit(solution)/shard_map/all_to_all | solution.py:117
  545.9 3.2 reduce.110
  551.9 8.4 %gather_fusion.7 = f32[2048,2,64]{2,1,0:T(2,128)S(1)} fusion(f32[2,2048,64]{2,0,1:T(2,128)} %bitcast.592, s32[2048]{0:T(1024)S(1)} %copy-done.20), kind=kCustom, calls=%fused_computation.7 | custom fusion | bytes 2105344 | tf_op jit(solution)/shard_map/gather | solution.py:129
  560.3 7.4 select_bitcast_fusion
  575.7 3.5 fusion.104
  579.5 7.2 all_to_all.103
  588.0 3.6 fusion.165
  591.7 4.5 multiply_reduce_fusion
  596.1 5.1 convolution_bitcast_fusion
  601.2 5.3 fusion.80
  606.9 7.2 all_to_all.104
  615.3 3.1 fusion.62
  625.4 14.4 %gather_fusion.8 = f32[2048,2,64]{2,1,0:T(2,128)} fusion(f32[2,2048,64]{2,0,1:T(2,128)S(1)} %copy.66, s32[2048]{0:T(1024)S(1)} %copy-done.18), kind=kCustom, calls=%fused_computation.8 | custom fusion | bytes 2105344 | tf_op jit(solution)/shard_map/gather | solution.py:87
  639.8 5.6 fusion.253
  647.6 22.9 %all_to_all.105 = f32[32,1,8192]{2,1,0:T(1,128)S(1)} all-to-all(f32[32,1,8192]{2,1,0:T(1,128)S(1)} %reshape.1347), channel_id=1, replica_groups=mesh['freq'=4,'tile'=32] {'tile'}, dimensions={0} | all-to-all | bytes 2097152 | tf_op jit(solution)/shard_map/all_to_all | solution.py:88
  670.6 3.2 reduce.113
  676.6 10.3 %gather_fusion.9 = f32[2048,2,64]{2,1,0:T(2,128)S(1)} fusion(f32[2,32,1,64,64]{4,0,3,2,1:T(2,128)} %bitcast.593, s32[2048]{0:T(1024)S(1)} %bitcast.566), kind=kCustom, calls=%fused_computation.9 | custom fusion | bytes 2121728 | tf_op jit(solution)/shard_map/gather | solution.py:95
  687.0 7.4 select_bitcast_fusion.2
  704.7 62.9 %all-reduce.1 = (f32[]{:T(128)}, f32[]{:T(128)}) all-reduce(f32[]{:T(128)} %get-tuple-element.242, f32[]{:T(128)} %fusion.167), channel_id=1, replica_groups=mesh['freq'=4,'tile'=32] {'freq','tile'}, use_global_device_ids=true, to_apply=%region_9.10 | all-reduce | flops 2 | bytes 16 | tf_op jit(solution)/shard_map/psum | solution.py:148
  769.0 8.5 %multiply_subtract_fusion = f32[64,64,256]{2,1,0:T(8,128)} fusion(f32[64,64,256]{2,1,0:T(8,128)} %copy-done.10, f32[64,64,256]{2,1,0:T(8,128)} %param.6, f32[64,64,256]{2,1,0:T(8,128)} %copy-done.9, f32[]{:T(128)S(6)} %div.7, f32[]{:T(128)S(6)} %div.6), kind=kLoop, calls=%fused_computation.10 | loop fusion | flops 4194304 | bytes 16777224 | tf_op jit(solution)/shard_map/sub | solution.py:153
  (202 shorter events, 118.9 us)
Async XLA Ops:
  0.6 7.4 copy-start.24
  0.6 7.4 copy-start.11
  8.1 11.3 %copy-start.13 = (s32[1,32,32]{2,1,0:T(8,128)S(1)}, s32[1,32,32]{2,1,0:T(8,128)}, u32[]{:S(2)}) copy-start(s32[1,32,32]{2,1,0:T(8,128)} %param.8) | copy-start | bytes 12292
  14.1 62.8 %all-to-all-start = ((f32[4,1,8192]{2,1,0:T(1,128)}), f32[4,1,8192]{2,1,0:T(1,128)S(1)}, u32[]{:S(2)}, u32[]{:S(2)}) async-start(f32[4,1,8192]{2,1,0:T(1,128)} %reshape.1329), calls=%async_computation | async-start | bytes 262144 | tf_op jit(solution)/shard_map/all_to_all | solution.py:79
  29.6 73.8 %copy-start.21 = (pred[32,64]{1,0:T(8,128)(4,1)}, pred[32,64]{1,0:T(8,128)(4,1)S(1)}, u32[]{:S(2)}) copy-start(pred[32,64]{1,0:T(8,128)(4,1)S(1)} %iota_compare_fusion.5) | copy-start | bytes 6148
  29.7 59.1 %copy-start.16 = (s32[2048]{0:T(1024)}, s32[2048]{0:T(1024)S(1)}, u32[]{:S(2)}) copy-start(s32[2048]{0:T(1024)S(1)} %broadcast_clamp_fusion.1) | copy-start | bytes 24580
  78.7 6.2 copy-start
  112.2 54.5 %all-to-all-start.1 = ((f32[32,1,8192]{2,1,0:T(1,128)}), f32[32,1,8192]{2,1,0:T(1,128)S(1)}, u32[]{:S(2)}, u32[]{:S(2)}) async-start(f32[32,1,8192]{2,1,0:T(1,128)} %reshape.1331), calls=%async_computation.1 | async-start | bytes 2097152 | tf_op jit(solution)/shard_map/all_to_all | solution.py:88
  166.7 16.4 %copy-start.29 = (pred[2048]{0:T(1024)(128)(4,1)}, pred[2048]{0:T(1024)(128)(4,1)S(1)}, u32[]{:S(2)}) copy-start(pred[2048]{0:T(1024)(128)(4,1)S(1)} %get-tuple-element.82) | copy-start | bytes 6148
  190.5 2.2 copy-start.5
  198.3 1.9 copy-start.12
  207.0 15.5 %copy-start.27 = (pred[32,64]{1,0:T(8,128)(4,1)S(1)}, pred[32,64]{1,0:T(8,128)(4,1)}, u32[]{:S(2)}) copy-start(pred[32,64]{1,0:T(8,128)(4,1)} %iota_compare_fusion.6) | copy-start | bytes 6148
  228.1 10.6 %copy-start.32 = (s32[2048,1]{0,1:T(1,128)S(1)}, s32[2048,1]{0,1:T(1,128)}, u32[]{:S(2)}) copy-start(s32[2048,1]{0,1:T(1,128)} %get-tuple-element.244) | copy-start | bytes 24580
  231.3 24.6 %all-to-all-start.2 = ((f32[32,1,8192]{2,1,0:T(1,128)}), f32[32,1,8192]{2,1,0:T(1,128)S(1)}, u32[]{:S(2)}, u32[]{:S(2)}) async-start(f32[32,1,8192]{2,1,0:T(1,128)} %reshape.1333), calls=%async_computation.2 | async-start | bytes 2097152 | tf_op jit(solution)/shard_map/all_to_all | solution.py:117
  238.7 23.2 %copy-start.19 = (s32[2048]{0:T(1024)}, s32[2048]{0:T(1024)S(1)}, u32[]{:S(2)}) copy-start(s32[2048]{0:T(1024)S(1)} %broadcast_clamp_fusion) | copy-start | bytes 24580
  261.9 8.4 %copy-start.33 = (pred[2048]{0:T(1024)(128)(4,1)S(1)}, pred[2048]{0:T(1024)(128)(4,1)}, u32[]{:S(2)}) copy-start(pred[2048]{0:T(1024)(128)(4,1)} %get-tuple-element.78) | copy-start | bytes 6148
  277.8 2.2 copy-start.1
  285.7 9.1 %copy-start.35 = (s32[64]{0:T(128)S(1)}, s32[64]{0:T(128)}, u32[]{:S(2)}) copy-start(s32[64]{0:T(128)} %param.7) | copy-start | bytes 772
  289.1 11.6 %copy-start.25 = (s32[4]{0:T(128)S(1)}, s32[4]{0:T(128)}, u32[]{:S(2)}) copy-start(s32[4]{0:T(128)} %copy-done.24) | copy-start | bytes 52
  290.1 9.3 %all-to-all-start.3 = ((f32[4,1,8192]{2,1,0:T(1,128)}), f32[4,1,8192]{2,1,0:T(1,128)S(1)}, u32[]{:S(2)}, u32[]{:S(2)}) async-start(f32[4,1,8192]{2,1,0:T(1,128)} %reshape.1335), calls=%async_computation.3 | async-start | bytes 262144 | tf_op jit(solution)/shard_map/all_to_all | solution.py:134
  294.9 9.6 %copy-start.14 = (f32[64,256]{1,0:T(8,128)}, f32[64,256]{1,0:T(8,128)S(1)}, u32[]{:S(2)}) copy-start(f32[64,256]{1,0:T(8,128)S(1)} %fusion.170) | copy-start | bytes 196612
  308.9 5.1 copy-start.9
  328.0 6.1 copy-start.2
  337.0 1.1 copy-start.17
  338.1 14.5 %copy-start.22 = (pred[32,64]{1,0:T(8,128)(4,1)S(1)}, pred[32,64]{1,0:T(8,128)(4,1)}, u32[]{:S(2)}) copy-start(pred[32,64]{1,0:T(8,128)(4,1)} %copy-done.21) | copy-start | bytes 6148
  388.5 17.6 %copy-start.30 = (pred[2048]{0:T(1024)(128)(4,1)S(1)}, pred[2048]{0:T(1024)(128)(4,1)}, u32[]{:S(2)}) copy-start(pred[2048]{0:T(1024)(128)(4,1)} %copy-done.29) | copy-start | bytes 6148
  416.1 2.2 copy-start.6
  490.9 6.1 copy-start.7
  500.9 15.1 %copy-start.28 = (pred[32,64]{1,0:T(8,128)(4,1)S(1)}, pred[32,64]{1,0:T(8,128)(4,1)}, u32[]{:S(2)}) copy-start(pred[32,64]{1,0:T(8,128)(4,1)} %iota_compare_fusion.6) | copy-start | bytes 6148
  549.1 2.9 copy-start.20
  551.9 8.4 %copy-start.34 = (pred[2048]{0:T(1024)(128)(4,1)S(1)}, pred[2048]{0:T(1024)(128)(4,1)}, u32[]{:S(2)}) copy-start(pred[2048]{0:T(1024)(128)(4,1)} %get-tuple-element.78) | copy-start | bytes 6148
  567.8 2.2 copy-start.3
  579.1 8.9 %copy-start.26 = (s32[4]{0:T(128)S(1)}, s32[4]{0:T(128)}, u32[]{:S(2)}) copy-start(s32[4]{0:T(128)} %copy-done.24) | copy-start | bytes 52
  588.0 3.6 copy-start.15
  596.1 5.1 copy-start.10
  615.3 6.1 copy-start.4
  624.3 1.1 copy-start.18
  625.4 14.4 %copy-start.23 = (pred[32,64]{1,0:T(8,128)(4,1)S(1)}, pred[32,64]{1,0:T(8,128)(4,1)}, u32[]{:S(2)}) copy-start(pred[32,64]{1,0:T(8,128)(4,1)} %copy-done.21) | copy-start | bytes 6148
  676.6 10.3 %copy-start.31 = (pred[2048]{0:T(1024)(128)(4,1)S(1)}, pred[2048]{0:T(1024)(128)(4,1)}, u32[]{:S(2)}) copy-start(pred[2048]{0:T(1024)(128)(4,1)} %copy-done.29) | copy-start | bytes 6148
  694.4 2.2 copy-start.8
where the time goes:
time: 787 us; the launch traced here: 778 us
  blocking collectives  216 us (27%)
  other arithmetic  184 us (23%)
  local copies, waits for them, and re-layouts  182 us (23%)
  matrix products  131 us (17%)
  starting transfers between devices  39 us (5%)
  waiting for transfers between devices  21.7 us (3%)
    psum x2, blocking collectives, body(): grad_norm = lax.psum(grad_norm_local, ('freq', 'tile'))  126 us
    all_to_all x2, blocking collectives, apply_here(): lax.all_to_all(packed, 'tile', split_axis=1, concat_axis=1, tiled=True)  46.3 us
    gather x3, local copies, waits for them, and re-layouts, apply_here(): column_contributions[:, source]  43.5 us
    dot_general x20, matrix products, mat_tmul(): lax.dot_general(left, right, (((0,), (0,)), ((), ())), precision=HIGH, pr...  41.1 us
    dot_general x20, matrix products, mat_mul(): jnp.dot(left, right, precision=HIGH, preferred_element_type=jnp.float32)  40.4 us
    gather x3, local copies, waits for them, and re-layouts, apply_here(): picked = arrived[:, which, 0, jnp.minimum(inner, kmax - 1)]  38.2 us
    lt x1, other arithmetic, body(): adjoint_live = adjoint_inner < ranks_col[adjoint_which]  31.9 us
    lt x1, other arithmetic, apply_here(): live = inner < rank_f[row][which]  31.4 us
  transfers between devices with their start and end apart: 4, of which 2 were waited for; matrix products, arithmetic and copies ran while one was open for 12% of the time, Pallas kernels for 0%

commit v1 on v0

v1 whole, which is shorter than its diff:
```python
import functools

import jax
import jax.numpy as jnp
import numpy as np
from jax import lax
from jax.experimental import pallas as pl
from jax.experimental.pallas import tpu as pltpu
from jax.sharding import PartitionSpec as P

FLO = 16
MESH = pl.DeviceIdType.MESH
F32, BF16 = jnp.float32, jnp.bfloat16
NF, NTILE, KMAX, NB, NV, NT, BLK = 4, 32, 64, 256, 64, 256, 64
NG = 8


def basis():
    steps = np.arange(NT)
    freqs = FLO + np.arange(NF)
    angle = (freqs[:, None] * steps[None, :] % NT).astype(np.float32) * np.float32(2.0 * np.pi / NT)
    return np.concatenate([np.cos(angle), -np.sin(angle)]).astype(np.float32)


def split(a):
    hi = a.astype(BF16)
    return hi, (a - hi.astype(F32)).astype(BF16)


def dot(a, b, dims=((1,), (0,))):
    return lax.dot_general(a, b, (dims, ((), ())), preferred_element_type=F32)


def swap(a):
    lane = lax.broadcasted_iota(jnp.int32, a.shape, 1)
    r = pltpu.roll(a, 64, 1)
    return jnp.where(lane < 64, r, -r)


def rhs(a, sign):
    b = sign * swap(a)
    ah, al = split(a)
    bh, bl = split(b)
    return jnp.concatenate([jnp.concatenate([ah, al], 1), jnp.concatenate([bh, bl], 1)], 0)


def three(o):
    return o[:256, :128] + o[:256, 128:] + o[256:, :128]


def setup_kernel(me_ref, ranks_ref, x_hbm, v_hbm, u_hbm, bb_ref, spec_ref, vt_hbm, ut_hbm, x_buf, raw, tall, packed, ld_sem, st_sem):
    me = me_ref[0]
    loads = []
    for m, hbm in enumerate((v_hbm, u_hbm)):
        for c in range(2):
            loads.append(pltpu.make_async_copy(hbm.at[c], raw.at[m, c], ld_sem.at[m * 2 + c]))
    loads.append(pltpu.make_async_copy(x_hbm, x_buf, ld_sem.at[4]))
    for cp in loads:
        cp.start()

    def flip(m):
        for c in range(2):
            loads[m * 2 + c].wait()

            @pl.loop(0, 16)
            def _(b):
                cols = pl.ds(pl.multiple_of(b * 128, 128), 128)
                turned = raw[m, c, :, cols].T
                tall[c, 0, cols, :] = turned[:, :128]
                tall[c, 1, cols, :] = turned[:, 128:]

    def store(m, g):
        return pltpu.make_async_copy(packed.at[m, g], (vt_hbm, ut_hbm)[m].at[g], st_sem.at[m, g])

    def pack(m, rank_at):
        def one(g, off):
            for j in range(4):
                k = rank_at(g * 4 + j)
                for c in range(2):
                    piece = jnp.concatenate([tall[c, h, pl.ds(off, 64), :] for h in range(2)], 1)
                    slot = lax.broadcasted_iota(jnp.int32, (64, NB), 0)
                    hi, lo = split(jnp.where(slot < k, piece, 0.0))
                    packed[m, g, j * 64:(j + 1) * 64, c * 256:(c + 1) * 256] = hi
                    packed[m, g, 256 + j * 64:256 + (j + 1) * 64, c * 256:(c + 1) * 256] = lo
                off = off + k
            store(m, g).start()
            return off

        lax.fori_loop(0, NG, one, jnp.int32(0))

    flip(0)
    pack(0, lambda i: ranks_ref[i, me])
    flip(1)
    pack(1, lambda j: ranks_ref[me, j])
    loads[4].wait()
    bb = bb_ref[...]

    @pl.loop(0, 16)
    def _(k):
        hi, lo = split(x_buf[pl.ds(pl.multiple_of(k * 256, 256), 256), :])
        o1 = dot(bb, hi, ((1,), (1,)))
        o2 = dot(bb, lo, ((1,), (1,)))
        o = o1[:8] + o1[8:] + o2[:8]
        for r in range(4):
            row = jnp.concatenate([o[:4, r * 64:(r + 1) * 64], o[4:, r * 64:(r + 1) * 64]], 1)
            spec_ref[pl.ds(k * 4 + r, 4, stride=64), :] = row

    for m in range(2):
        @pl.loop(0, NG)
        def _(g):
            store(m, g).wait()


def main_kernel(
    mute_ref, spec_ref, vt_hbm, ut_hbm, data_ref, prod_ref,
    comb_ref, resid_ref,
    vt, vn, ut, un, wbuf, zbuf, fsend, frecv, spec0, right, acc,
    gmap, r0_ref, im_ref, sc_send, sc_recv, sc2_send, sc2_recv,
    ld_sem, ts_sem, tr_sem, fs_sem, fr_sem, ss_sem, sr_sem, s2s_sem, s2r_sem,
):
    me = lax.axis_index("tile")
    fme = lax.axis_index("freq")
    mygroup = me // 4

    loads = [pltpu.make_async_copy(vt_hbm, vt, ld_sem.at[0]), pltpu.make_async_copy(ut_hbm, ut, ld_sem.at[1])]
    for cp in loads:
        cp.start()

    def setup_wide(t_ref, n_ref):
        @pl.loop(0, NG)
        def _(g):
            for p in range(2):
                for c in range(2):
                    n_ref[g, p * 256:(p + 1) * 256, c * 256:(c + 1) * 256] = (
                        t_ref[g, p * 256:(p + 1) * 256, c * 256:(c + 1) * 256].T)

    bar = pltpu.get_barrier_semaphore()

    @pl.loop(1, NTILE)
    def _(d):
        pl.semaphore_signal(bar, inc=1, device_id={"tile": lax.rem(me + d, NTILE)}, device_id_type=MESH)

    for d in range(1, NF):
        pl.semaphore_signal(bar, inc=1, device_id={"freq": lax.rem(fme + d, NF)}, device_id_type=MESH)

    fsend[0] = spec_ref[...]
    pl.semaphore_wait(bar, NTILE - 1 + NF - 1)

    def fcopy(e, peer, at):
        return pltpu.make_async_remote_copy(
            src_ref=fsend.at[e, pl.ds(pl.multiple_of(peer * 64, 64), 64)],
            dst_ref=frecv.at[e, pl.ds(pl.multiple_of(at * 64, 64), 64)],
            send_sem=fs_sem.at[e, peer], recv_sem=fr_sem.at[e, at],
            device_id={"freq": peer}, device_id_type=MESH)

    def fstart(e):
        for d in range(1, NF):
            fcopy(e, lax.rem(fme + d, NF), fme).start()

    def fwait(e):
        for d in range(1, NF):
            peer = lax.rem(fme + d, NF)
            fcopy(e, peer, peer).wait()
        own = pl.ds(pl.multiple_of(fme * 64, 64), 64)
        frecv[e, own, :] = fsend[e, own, :]

    fstart(0)

    def tcopy(e, peer, at):
        return pltpu.make_async_remote_copy(
            src_ref=wbuf.at[e, peer], dst_ref=zbuf.at[e, at],
            send_sem=ts_sem.at[e, peer], recv_sem=tr_sem.at[e, at],
            device_id={"tile": peer}, device_id_type=MESH)

    inner = lax.rem(me, 4)

    def mate(d):
        return mygroup * 4 + lax.rem(inner + d, 4)

    def send_products(e, t_ref):
        def products(g):
            w = three(dot(t_ref[g], right[...]))
            for j in range(4):
                wbuf[e, g * 4 + j] = w[j * 64:(j + 1) * 64]

        products(mygroup)
        for d in range(1, 4):
            tcopy(e, mate(d), me).start()

        @pl.loop(1, NG)
        def _(k):
            g = lax.rem(mygroup + k, NG)
            products(g)
            for j in range(4):
                tcopy(e, g * 4 + j, me).start()

    def gather_products(e, n_ref):
        for d in range(1, 4):
            tcopy(e, mate(d), mate(d)).wait_recv()
        zbuf[e, me] = wbuf[e, me]
        z = zbuf[e, pl.ds(mygroup * 4, 4)].reshape(256, 128)
        acc[...] = dot(n_ref[mygroup], rhs(z, -1.0))

        @pl.loop(1, NG)
        def _(k):
            g = lax.rem(mygroup + NG - k, NG)
            for j in range(4):
                tcopy(e, g * 4 + j, g * 4 + j).wait_recv()
            z = zbuf[e, pl.ds(g * 4, 4)].reshape(256, 128)
            acc[...] += dot(n_ref[g], rhs(z, -1.0))

        return three(acc[...])

    def sent(e):
        @pl.loop(1, NTILE)
        def _(d):
            peer = lax.rem(me + d, NTILE)
            tcopy(e, peer, peer).wait_send()

    def scopy(n, peer, at):
        return pltpu.make_async_remote_copy(
            src_ref=sc_send.at[n], dst_ref=sc_recv.at[n, at],
            send_sem=ss_sem.at[n, peer], recv_sem=sr_sem.at[n, at],
            device_id={"tile": peer}, device_id_type=MESH)

    def s2copy(n, peer, at):
        return pltpu.make_async_remote_copy(
            src_ref=sc2_send.at[n], dst_ref=sc2_recv.at[n, at],
            send_sem=s2s_sem.at[n, peer], recv_sem=s2r_sem.at[n, at],
            device_id={"freq": peer}, device_id_type=MESH)

    def sum_start(n, gn, im):
        row = lax.broadcasted_iota(jnp.int32, (8, 128), 0)
        inn = jnp.sum(im * im, axis=0, keepdims=True)
        mine = jnp.where(row == 0, gn, jnp.where(row == 1, inn, 0.0))
        sc_send[n] = mine

        @pl.loop(1, NTILE)
        def _(d):
            scopy(n, lax.rem(me + d, NTILE), me).start()

    def sum_middle(n):
        @pl.loop(1, NTILE)
        def _(d):
            peer = lax.rem(me + d, NTILE)
            scopy(n, peer, peer).wait()

        sc_recv[n, me] = sc_send[n]
        part = jnp.sum(sc_recv[n], axis=0)
        sc2_send[n] = part
        for d in range(1, NF):
            s2copy(n, lax.rem(fme + d, NF), fme).start()

    def sum_end(n):
        for d in range(1, NF):
            peer = lax.rem(fme + d, NF)
            s2copy(n, peer, peer).wait()
        sc2_recv[n, fme] = sc2_send[n]
        both = jnp.sum(jnp.sum(sc2_recv[n], axis=0), axis=1, keepdims=True)
        return both[0:1] / both[1:2]

    def setup_gram():
        t = lax.broadcasted_iota(jnp.int32, (BLK, NT), 1)
        keep = (t >= mute_ref[...]).astype(F32)
        gram = jnp.dot(keep, prod_ref[...], precision=lax.Precision.HIGHEST, preferred_element_type=F32)
        lane = lax.broadcasted_iota(jnp.int32, (BLK, 128), 1)
        for fo in range(NF):
            for fi in range(NF):
                def col(a, b):
                    return jnp.broadcast_to(gram[:, a * 8 + b:a * 8 + b + 1], (BLK, 128))
                gmap[fo, fi, 0] = jnp.where(lane < 64, col(fo, fi), col(4 + fo, 4 + fi))
                gmap[fo, fi, 1] = jnp.where(lane < 64, col(fo, 4 + fi), col(4 + fo, fi))

    def mix(e_out, spec):
        rolled = [pltpu.roll(s, 64, 1) for s in spec]
        total = jnp.zeros((1, 128), F32)
        for fo in range(NF):
            o = jnp.zeros((BLK, 128), F32)
            for fi in range(NF):
                o += gmap[fo, fi, 0] * spec[fi] + gmap[fo, fi, 1] * rolled[fi]
            fsend[e_out, pl.ds(fo * 64, 64), :] = o
            total += jnp.sum(spec[fo] * o, axis=0, keepdims=True)
        return total

    def read_spec(e):
        return [frecv[e, pl.ds(f * 64, 64), :] for f in range(NF)]

    loads[0].wait()
    fwait(0)
    right[...] = rhs(frecv[0], 1.0)
    send_products(0, vt)
    loads[1].wait()
    setup_wide(ut, un)
    r0 = gather_products(0, un) - jnp.concatenate([data_ref[0], data_ref[1]], 1)
    r0_ref[...] = r0

    right[...] = rhs(r0, 1.0)
    send_products(1, ut)
    setup_wide(vt, vn)
    setup_gram()
    fsend[1] = gather_products(1, vn)
    fstart(1)
    fwait(1)
    s0 = read_spec(1)
    gn0 = mix(2, s0)
    fstart(2)
    for f in range(NF):
        spec0[f] = s0[f]
    fwait(2)
    right[...] = rhs(frecv[2], 1.0)
    send_products(2, vt)
    im0 = gather_products(2, un)
    im_ref[...] = im0
    sum_start(0, gn0, im0)

    right[...] = rhs(im0, 1.0)
    send_products(3, ut)
    sum_middle(0)
    fsend[3] = gather_products(3, vn)
    fstart(3)
    alpha0 = sum_end(0)
    fwait(3)
    q = read_spec(3)
    s1 = [spec0[f] - alpha0 * q[f] for f in range(NF)]
    gn1 = mix(4, s1)
    fstart(4)
    for f in range(NF):
        comb_ref[pl.ds(f * 64, 64), :] = s1[f]
    fwait(4)
    right[...] = rhs(frecv[4], 1.0)
    send_products(4, vt)
    im1 = gather_products(4, un)
    sum_start(1, gn1, im1)
    for e in range(5):
        sent(e)
    part = r0_ref[...] - alpha0 * im_ref[...]
    sum_middle(1)
    alpha1 = sum_end(1)
    out = part - alpha1 * im1
    resid_ref[0] = out[:, :64]
    resid_ref[1] = out[:, 64:]
    for f in range(NF):
        rows = pl.ds(f * 64, 64)
        comb_ref[rows, :] = alpha0 * spec0[f] + alpha1 * comb_ref[rows, :]


def final_kernel(mute_ref, comb_ref, b3_ref, x_ref, o_ref):
    g = pl.program_id(0)
    nr = x_ref.shape[0]
    b3 = b3_ref[...]
    t = lax.broadcasted_iota(jnp.int32, (NV, NT), 1)
    for p in range(0, nr, 2):
        cols = []
        for r in (p, p + 1):
            row = comb_ref[pl.ds(g * nr + r, 4, stride=64), :]
            cols.append(jnp.concatenate([row[:, :64], row[:, 64:]], 0))
        c = jnp.concatenate(cols, 1)
        hi, lo = split(c)
        hi, lo = hi.astype(F32), lo.astype(F32)
        lhs = jnp.concatenate([hi, lo, hi, jnp.zeros_like(hi)], 0)
        grad = dot(lhs.T.astype(BF16), b3)
        for i, r in enumerate((p, p + 1)):
            o_ref[r] = x_ref[r] - jnp.where(t >= mute_ref[g * nr + r], grad[i * 64:(i + 1) * 64], 0.0)


def body(x_time, mute, ranks, right_factor_columns, u_rows, data):
    b = basis()
    bj = jnp.asarray(b)
    bhi, blo = split(bj)
    bb = jnp.concatenate([bhi, blo], 0)
    b3 = jnp.concatenate([bhi, bhi, blo, jnp.zeros_like(bhi)], 0)
    prod = jnp.asarray((b[:, None, :] * b[None, :, :]).reshape(64, NT).T)
    prod = jnp.pad(prod, ((0, 0), (0, 64)))
    vmem = pl.BlockSpec(memory_space=pltpu.VMEM)
    hbm = pl.BlockSpec(memory_space=pl.ANY)
    smem = pl.BlockSpec(memory_space=pltpu.SMEM)
    dma = pltpu.SemaphoreType.DMA
    packed = jax.ShapeDtypeStruct((NG, 512, 512), BF16)
    spec, vt, ut = pl.pallas_call(
        setup_kernel,
        out_shape=(jax.ShapeDtypeStruct((256, 128), F32), packed, packed),
        in_specs=[smem, smem, hbm, hbm, hbm, vmem],
        out_specs=(vmem, hbm, hbm),
        scratch_shapes=[
            pltpu.VMEM((4096, 256), F32),
            pltpu.VMEM((2, 2, 256, 2048), F32),
            pltpu.VMEM((2, 2, 2048, 128), F32),
            pltpu.VMEM((2, NG, 512, 512), BF16),
            dma((5,)), dma((2, NG)),
        ],
        compiler_params=pltpu.CompilerParams(vmem_limit_bytes=40 << 20),
        name="setup",
    )(lax.axis_index("tile").reshape(1), ranks[0], x_time.reshape(4096, 256), right_factor_columns[0, :, 0], u_rows[0, :, 0], bb)
    comb, resid = pl.pallas_call(
        main_kernel,
        out_shape=(jax.ShapeDtypeStruct((256, 128), F32), jax.ShapeDtypeStruct((2, 256, 64), F32)),
        in_specs=[vmem, vmem, hbm, hbm, vmem, vmem],
        out_specs=(vmem, vmem),
        scratch_shapes=[
            pltpu.VMEM((NG, 512, 512), BF16),
            pltpu.VMEM((NG, 512, 512), BF16),
            pltpu.VMEM((NG, 512, 512), BF16),
            pltpu.VMEM((NG, 512, 512), BF16),
            pltpu.VMEM((5, NTILE, 64, 128), F32),
            pltpu.VMEM((5, NTILE, 64, 128), F32),
            pltpu.VMEM((5, 256, 128), F32),
            pltpu.VMEM((5, 256, 128), F32),
            pltpu.VMEM((NF, 64, 128), F32),
            pltpu.VMEM((512, 256), BF16),
            pltpu.VMEM((512, 256), F32),
            pltpu.VMEM((NF, NF, 2, BLK, 128), F32),
            pltpu.VMEM((256, 128), F32),
            pltpu.VMEM((256, 128), F32),
            pltpu.VMEM((2, 8, 128), F32),
            pltpu.VMEM((2, NTILE, 8, 128), F32),
            pltpu.VMEM((2, 8, 128), F32),
            pltpu.VMEM((2, NF, 8, 128), F32),
            dma((2,)), dma((5, NTILE)), dma((5, NTILE)), dma((5, NF)), dma((5, NF)),
            dma((2, NTILE)), dma((2, NTILE)), dma((2, NF)), dma((2, NF)),
        ],
        compiler_params=pltpu.CompilerParams(collective_id=0, has_side_effects=True, vmem_limit_bytes=56 << 20),
        name="descent",
    )(mute[:, None], spec, vt, ut, data[0], prod)
    step = 16
    x_out = pl.pallas_call(
        final_kernel,
        grid=(BLK // step,),
        out_shape=jax.ShapeDtypeStruct((BLK, NV, NT), F32),
        in_specs=[
            smem, vmem, vmem,
            pl.BlockSpec((step, NV, NT), lambda i: (i, 0, 0)),
        ],
        out_specs=pl.BlockSpec((step, NV, NT), lambda i: (i, 0, 0)),
        compiler_params=pltpu.CompilerParams(vmem_limit_bytes=32 << 20),
        name="update",
    )(mute, comb, b3, x_time)
    return x_out, resid[None]


def solution(mesh):
    in_specs = (
        P(("tile", "freq"), None, None),
        P(("tile", "freq")),
        P("freq", None, None),
        P("freq", None, "tile", None, None),
        P("freq", None, "tile", None, None),
        P("freq", None, "tile", None),
    )
    out_specs = (P(("tile", "freq"), None, None), P("freq", None, "tile", None))
    return jax.shard_map(body, mesh=mesh, in_specs=in_specs, out_specs=out_specs, check_vma=False)
```

time: 787 us -> 162 us (0.21); the launches traced: 778 us -> 161 us
  blocking collectives: 216 us -> 0 us
  other arithmetic: 184 us -> 0 us
  local copies, waits for them, and re-layouts: 182 us -> 16.1 us
  Pallas kernels: 0 us -> 145 us
  matrix products: 131 us -> 0 us
  starting transfers between devices: 39 us -> 0 us
  waiting for transfers between devices: 21.7 us -> 0 us
    pallas_call x0 -> x3, Pallas kernels: none -> 145 us  [the longest x1 125 us: body(): pl.pallas_call(main_kernel, out_shape=(jax.ShapeDtypeStruct((256, 128), F...]
    gather x18 -> x0, local copies, waits for them, and re-layouts: 135 us -> none  [the longest x3 43.5 us: apply_here(): column_contributions[:, source]]
    dot_general x50 -> x0, matrix products: 131 us -> none  [the longest x20 41.1 us: mat_tmul(): lax.dot_general(left, right, (((0,), (0,)), ((), ())), precision=HIGH, pr...]
    psum x2 -> x0, blocking collectives: 126 us -> none  [body(): grad_norm = lax.psum(grad_norm_local, ('freq', 'tile'))]
    all_to_all x6 -> x0, blocking collectives: 89.9 us -> none  [the longest x2 46.3 us: apply_here(): lax.all_to_all(packed, 'tile', split_axis=1, concat_axis=1, tiled=True)]
    lt x4 -> x0, other arithmetic: 64.1 us -> none  [the longest x1 31.9 us: body(): adjoint_live = adjoint_inner < ranks_col[adjoint_which]]
    select_n x6 -> x0, other arithmetic: 39.8 us -> none  [the longest x3 24.9 us: apply_here(): collected_pieces = jnp.where(live[None, :, None], picked, 0.0)]
    all_to_all x4 -> x0, starting transfers between devices: 39 us -> none  [the longest x1 21.7 us: apply_here(): lax.all_to_all(packed, 'tile', split_axis=1, concat_axis=1, tiled=True)]
  transfers between devices with their start and end apart: 4 -> 0, of which waited for: 2 -> 0; matrix products, arithmetic and copies ran while one was open for 12% -> 0% of each run, Pallas kernels for 0% -> 0%
where the time goes in v1:
time: 162 us; the launch traced here: 161 us
  Pallas kernels  145 us (90%)
  local copies, waits for them, and re-layouts  16.1 us (10%)
    pallas_call x1, Pallas kernels, body(): pl.pallas_call(main_kernel, out_shape=(jax.ShapeDtypeStruct((256, 128), F...  125 us
    pallas_call x1, Pallas kernels, body(): pl.pallas_call(setup_kernel, out_shape=(jax.ShapeDtypeStruct((256, 128),...  15.4 us
    unnamed x22, local copies, waits for them, and re-layouts  14.8 us
    pallas_call x1, Pallas kernels, body(): pl.pallas_call(final_kernel, grid=(BLK // step,), out_shape=jax.ShapeDtyp...  4.12 us

profile of v1, /device:TPU:1, one launch (start us, length us, event | category | flops | bytes accessed | tf_op | source)
XLA Modules:
  0.0 161.3 jit_solution(12963880125848244565)
XLA Ops:
  0.6 1.3 copy.11.mute_ref
  2.0 1.7 %copy.10 = f32[1,2,256,64]{3,2,1,0:T(8,128)} copy(f32[1,2,256,64]{2,3,1,0:T(8,128)} %param.13) | data formatting | bytes 262144 | tf_op args[5]
  3.7 0.0 copy-start
  3.7 2.2 %copy-done = f32[64,64,256]{2,1,0:T(8,128)S(1)} copy-done((f32[64,64,256]{2,1,0:T(8,128)S(1)}, f32[64,64,256]{2,1,0:T(8,128)}, u32[]{:S(2)}) %copy-start) | copy-done | bytes 4194328
  5.9 0.0 copy-start.6
  5.9 0.7 copy-done.6
  6.6 0.0 copy-start.8
  6.6 0.7 copy-done.8
  7.3 15.4 %setup.1 = (f32[256,128]{1,0:T(8,128)S(1)}, bf16[8,512,512]{2,1,0:T(8,128)(2,1)S(1)}, bf16[8,512,512]{2,1,0:T(8,128)(2,1)S(1)}) custom-call(s32[1]{0:T(128)} %bitcast.1.me_ref, s32[32,32]{1,0:T(8,128)S(1)} %bitcast.9, f32[4096,256]{1,0:T(8,128)S(1)} %bitcast.8, f32[2,256,2048]{2,1,0:T(8,128)} %bitcast.11, f32[2,256,2048]{2,1,0:T(8,128)} %bitcast.12, ...), custom_call_target="tpu_custom_call" | custom-call | tf_op jit(solution)/shard_map/setup/pallas_call | solution.py:379
  22.7 0.0 copy-start.2
  22.8 2.0 %copy-done.2 = bf16[8,512,512]{2,1,0:T(8,128)(2,1)} copy-done((bf16[8,512,512]{2,1,0:T(8,128)(2,1)}, bf16[8,512,512]{2,1,0:T(8,128)(2,1)S(1)}, u32[]{:S(2)}) %copy-start.2) | copy-done | bytes 4194328
  24.8 0.0 copy-start.3
  24.8 2.0 %copy-done.3 = bf16[8,512,512]{2,1,0:T(8,128)(2,1)} copy-done((bf16[8,512,512]{2,1,0:T(8,128)(2,1)}, bf16[8,512,512]{2,1,0:T(8,128)(2,1)S(1)}, u32[]{:S(2)}) %copy-start.3) | copy-done | bytes 4194328
  26.7 0.0 copy-start.4
  26.7 0.7 copy-done.4
  27.4 0.0 copy-start.7
  27.4 0.0 copy-start.9
  27.4 125.0 %descent.1 = (f32[256,128]{1,0:T(8,128)}, f32[2,256,64]{2,1,0:T(8,128)}) custom-call(s32[64,1]{1,0:T(8,128)} %copy.11.mute_ref, f32[256,128]{1,0:T(8,128)} %copy-done.4, bf16[8,512,512]{2,1,0:T(8,128)(2,1)} %copy-done.2, bf16[8,512,512]{2,1,0:T(8,128)(2,1)} %copy-done.3, f32[2,256,64]{2,1,0:T(8,128)} %bitcast.13, f32[256,128]{1,0:T(8,128)} %constant.28.prod_ref), custom_call_target="tpu_custom_call" | custom-call | tf_op jit(solution)/shard_map/descent/pallas_call | solution.py:394
  152.4 1.7 %copy.12 = f32[1,2,256,64]{2,3,1,0:T(8,128)} copy(f32[1,2,256,64]{3,2,1,0:T(8,128)} %bitcast.14) | data formatting | bytes 262144
  154.1 0.0 copy-done.7
  154.1 0.0 copy-done.9
  154.1 0.0 copy-start.1
  154.1 2.2 %copy-done.1 = f32[64,64,256]{2,1,0:T(8,128)S(1)} copy-done((f32[64,64,256]{2,1,0:T(8,128)S(1)}, f32[64,64,256]{2,1,0:T(8,128)}, u32[]{:S(2)}) %copy-start.1) | copy-done | bytes 4194328
  156.3 0.0 copy-start.5
  156.3 0.9 copy-done.5
  157.2 4.1 %update.1 = f32[64,64,256]{2,1,0:T(8,128)} custom-call(s32[64]{0:T(128)S(1)} %copy-done.9, f32[256,128]{1,0:T(8,128)S(1)} %copy-done.5, bf16[32,256]{1,0:T(8,128)(2,1)S(1)} %copy-done.7, f32[64,64,256]{2,1,0:T(8,128)S(1)} %copy-done.1), custom_call_target="tpu_custom_call" | custom-call | tf_op jit(solution)/shard_map/update/pallas_call | solution.py:425
Async XLA Ops:
  3.7 2.2 %copy-start = (f32[64,64,256]{2,1,0:T(8,128)S(1)}, f32[64,64,256]{2,1,0:T(8,128)}, u32[]{:S(2)}) copy-start(f32[64,64,256]{2,1,0:T(8,128)} %x_ref.1) | copy-start | bytes 12582916
  5.9 0.7 copy-start.6
  6.6 0.7 copy-start.8
  22.7 2.0 %copy-start.2 = (bf16[8,512,512]{2,1,0:T(8,128)(2,1)}, bf16[8,512,512]{2,1,0:T(8,128)(2,1)S(1)}, u32[]{:S(2)}) copy-start(bf16[8,512,512]{2,1,0:T(8,128)(2,1)S(1)} %get-tuple-element.8.vt_hbm) | copy-start | bytes 12582916
  24.8 2.0 %copy-start.3 = (bf16[8,512,512]{2,1,0:T(8,128)(2,1)}, bf16[8,512,512]{2,1,0:T(8,128)(2,1)S(1)}, u32[]{:S(2)}) copy-start(bf16[8,512,512]{2,1,0:T(8,128)(2,1)S(1)} %get-tuple-element.9.ut_hbm) | copy-start | bytes 12582916
  26.7 0.7 copy-start.4
  27.4 126.7 %copy-start.7 = (bf16[32,256]{1,0:T(8,128)(2,1)S(1)}, bf16[32,256]{1,0:T(8,128)(2,1)}, u32[]{:S(2)}) copy-start(bf16[32,256]{1,0:T(8,128)(2,1)} %constant.29.b3_ref) | copy-start | bytes 49156
  27.4 126.7 %copy-start.9 = (s32[64]{0:T(128)S(1)}, s32[64]{0:T(128)}, u32[]{:S(2)}) copy-start(s32[64]{0:T(128)} %mute_ref.1) | copy-start | bytes 772
  154.1 2.2 %copy-start.1 = (f32[64,64,256]{2,1,0:T(8,128)S(1)}, f32[64,64,256]{2,1,0:T(8,128)}, u32[]{:S(2)}) copy-start(f32[64,64,256]{2,1,0:T(8,128)} %x_ref.1) | copy-start | bytes 12582916
  156.3 0.9 copy-start.5

commit v2 on v1

v2 whole, which is shorter than its diff:
```python
import jax
import jax.numpy as jnp
import numpy as np
from jax import lax
from jax.experimental import pallas as pl
from jax.experimental.pallas import tpu as pltpu
from jax.sharding import PartitionSpec as P

FLO = 16
MESH = pl.DeviceIdType.MESH
F32, BF16 = jnp.float32, jnp.bfloat16
NF, NTILE, NB, NV, NT, BLK = 4, 32, 256, 64, 256, 64
NG = 8
ROOM = 60 << 20

FIRST = ((2, 2), (2, 1), (1, 2), (1, 1), (1, 3), (2, 0), (1, 0), (0, 1))
SECOND = ((0, 0), (2, 3), (3, 2), (3, 3), (3, 1), (0, 2), (3, 0), (0, 3))
OWN = 2


def basis():
    steps = np.arange(NT)
    freqs = FLO + np.arange(NF)
    angle = (freqs[:, None] * steps[None, :] % NT).astype(np.float32) * np.float32(2.0 * np.pi / NT)
    return np.concatenate([np.cos(angle), -np.sin(angle)]).astype(np.float32)


def split(a):
    hi = a.astype(BF16)
    return hi, (a - hi.astype(F32)).astype(BF16)


def dot(a, b, dims=((1,), (0,))):
    return lax.dot_general(a, b, (dims, ((), ())), preferred_element_type=F32)


def lanes(shape):
    return lax.broadcasted_iota(jnp.int32, shape, 1)


def even(shape):
    return lax.rem(lanes(shape), 64) < 32


def swap(p):
    return jnp.where(even(p.shape), pltpu.roll(p, 96, 1), pltpu.roll(p, 32, 1))


def rhs(p, sign):
    left = lanes(p.shape) < 64
    s = swap(p)
    out = []
    for q in (p, jnp.where(even(p.shape), sign * s, -sign * s)):
        hi = q.astype(BF16).astype(F32)
        lo = q - hi
        out.append(jnp.where(left, hi, pltpu.roll(lo, 64, 1)).astype(BF16))
        out.append(jnp.where(left, pltpu.roll(hi, 64, 1), lo).astype(BF16))
    return jnp.concatenate(out, 0)


def pack(o):
    s = o[:256] + o[256:]
    s = s + pltpu.roll(s, 64, 1)
    return jnp.where(lanes((128, 128)) < 64, s[:128], s[128:])


def setup_kernel(me_ref, perm_ref, ranks_ref, x_hbm, v_hbm, u_hbm, bb_ref, spec_ref, vt_hbm, ut_hbm, x_buf, raw, tall, packed, offs, ld_sem, st_sem):
    me = me_ref[0]
    loads = [pltpu.make_async_copy(x_hbm, x_buf, ld_sem.at[4])]
    for m, hbm in enumerate((v_hbm, u_hbm)):
        for c in range(2):
            loads.append(pltpu.make_async_copy(hbm.at[c], raw.at[m, c], ld_sem.at[m * 2 + c]))
    for cp in loads:
        cp.start()

    def offsets(m, rank_at):
        def one(i, off):
            offs[m, i] = off
            return off + rank_at(i)

        lax.fori_loop(0, NTILE, one, jnp.int32(0))

    ranks_at = (lambda i: ranks_ref[i, me]), (lambda j: ranks_ref[me, j])
    offsets(0, ranks_at[0])
    offsets(1, ranks_at[1])

    def flip(m):
        for c in range(2):
            loads[1 + m * 2 + c].wait()

            @pl.loop(0, 16)
            def _(b):
                cols = pl.ds(pl.multiple_of(b * 128, 128), 128)
                order = [64 * i for i in range(4)] + [64 * i + 32 for i in range(4)]
                turned = jnp.concatenate([raw[m, c, i:i + 32, cols] for i in order], 0).T
                tall[c, 0, cols, :] = turned[:, :128]
                tall[c, 1, cols, :] = turned[:, 128:]

    def store(m, g):
        return pltpu.make_async_copy(packed.at[m, g], (vt_hbm, ut_hbm)[m].at[g], st_sem.at[m, g])

    def pad(m):
        @pl.loop(0, NG)
        def _(g):
            for j in range(4):
                tile = perm_ref[g * 4 + j]
                k = ranks_at[m](tile)
                off = offs[m, tile]
                for c in range(2):
                    piece = jnp.concatenate([tall[c, h, pl.ds(off, 64), :] for h in range(2)], 1)
                    slot = lax.broadcasted_iota(jnp.int32, (64, NB), 0)
                    for n, part in enumerate(split(jnp.where(slot < k, piece, 0.0))):
                        for h in range(2):
                            at = n * 256 + h * 128 + j * 32
                            packed[m, g, at:at + 32, c * 256:(c + 1) * 256] = part[h * 32:(h + 1) * 32]
            store(m, g).start()

    loads[0].wait()
    bb = bb_ref[...]
    quarter = even((4, 128))

    @pl.loop(0, BLK // 4)
    def _(k):
        low = pl.multiple_of(k * 128, 128)
        a, b = x_buf[pl.ds(low, 128), :], x_buf[pl.ds(BLK * 32 + low, 128), :]
        hi, lo = split(jnp.concatenate([a[:64], b[:64], a[64:], b[64:]], 0))
        o1 = dot(bb, hi, ((1,), (1,)))
        o2 = dot(bb, lo, ((1,), (1,)))
        o = o1[:8] + o1[8:] + o2[:8]
        for i in range(2):
            re, im = o[:4, i * 128:(i + 1) * 128], o[4:, i * 128:(i + 1) * 128]
            rows = pl.ds(k * 2 + i, 4, stride=32)
            spec_ref[0, rows, :] = jnp.where(quarter, re, pltpu.roll(im, 32, 1))
            spec_ref[1, rows, :] = jnp.where(quarter, pltpu.roll(re, 96, 1), im)

    for m in range(2):
        flip(m)
        pad(m)
    for m in range(2):
        @pl.loop(0, NG)
        def _(g):
            store(m, g).wait()


def main_kernel(
    mute_ref, spec_ref, vt_hbm, ut_hbm, data_ref, prod_ref,
    comb_ref, resid_ref,
    vt, vn, ut, un, wbuf, zbuf, fsend, frecv, spec0, right, acc,
    keep_ref, gmap, r0_ref, im_ref, gn_ref, sc_send, sc_recv, sc2_send, sc2_recv,
    ld_sem, ts_sem, tr_sem, fs_sem, fr_sem, ss_sem, sr_sem, s2s_sem, s2r_sem,
):
    me = lax.axis_index("tile")
    fme = lax.axis_index("freq")
    my_z, my_y, my_c = me // 8, lax.rem(me // 2, 4), lax.rem(me, 2)

    loads = [pltpu.make_async_copy(vt_hbm, vt, ld_sem.at[0]), pltpu.make_async_copy(ut_hbm, ut, ld_sem.at[1])]
    for cp in loads:
        cp.start()

    bar = pltpu.get_barrier_semaphore()

    @pl.loop(1, NTILE)
    def _(d):
        pl.semaphore_signal(bar, inc=1, device_id={"tile": lax.rem(me + d, NTILE)}, device_id_type=MESH)

    for d in range(1, NF):
        pl.semaphore_signal(bar, inc=1, device_id={"freq": lax.rem(fme + d, NF)}, device_id_type=MESH)

    def setup_wide(t_ref, n_ref):
        @pl.loop(0, NG)
        def _(g):
            for p in range(2):
                for c in range(2):
                    n_ref[g, p * 256:(p + 1) * 256, c * 256:(c + 1) * 256] = (
                        t_ref[g, p * 256:(p + 1) * 256, c * 256:(c + 1) * 256].T)

    def fcopy(e, h, peer, at):
        return pltpu.make_async_remote_copy(
            src_ref=fsend.at[e, h, pl.ds(pl.multiple_of(peer * 32, 32), 32)],
            dst_ref=frecv.at[e, h, pl.ds(pl.multiple_of(at * 32, 32), 32)],
            send_sem=fs_sem.at[e, h, peer], recv_sem=fr_sem.at[e, h, at],
            device_id={"freq": peer}, device_id_type=MESH)

    def fstart(e, h):
        for d in (2, 1, 3):
            fcopy(e, h, lax.rem(fme + d, NF), fme).start()

    def fwait(e, h):
        for d in range(1, NF):
            peer = lax.rem(fme + d, NF)
            fcopy(e, h, peer, peer).wait()
        own = pl.ds(pl.multiple_of(fme * 32, 32), 32)
        frecv[e, h, own, :] = fsend[e, h, own, :]

    def offset(g, half):
        table = (FIRST, SECOND)[half]
        dz, dy = jnp.int32(table[0][0]), jnp.int32(table[0][1])
        for i in range(1, NG):
            dz, dy = jnp.where(g == i, table[i][0], dz), jnp.where(g == i, table[i][1], dy)
        return dz, dy

    def tcopy(e, h, g, j):
        half, dc = j // 2, j % 2
        dz, dy = offset(g, half)
        peer = lax.rem(my_z + dz, 4) * 8 + lax.rem(my_y + dy, 4) * 2 + lax.rem(my_c + dc, 2)
        same = jnp.logical_or(g == 0, g == 5)
        slot = g * 4 + jnp.where(same, half, 1 - half) * 2 + dc
        return pltpu.make_async_remote_copy(
            src_ref=wbuf.at[e, h, g * 4 + j], dst_ref=zbuf.at[e, h, slot],
            send_sem=ts_sem.at[e, h, g * 4 + j], recv_sem=tr_sem.at[e, h, slot],
            device_id={"tile": peer}, device_id_type=MESH)

    def arrival(e, h, p):
        return pltpu.make_async_remote_copy(
            src_ref=wbuf.at[e, h, p], dst_ref=zbuf.at[e, h, p],
            send_sem=ts_sem.at[e, h, p], recv_sem=tr_sem.at[e, h, p],
            device_id={"tile": lax.rem(me + 1, NTILE)}, device_id_type=MESH)

    def send_products(e, h, t_ref, p, sign=1.0):
        right[...] = rhs(p, sign)

        @pl.loop(0, NG // 2)
        def _(k):
            o = dot(t_ref[pl.ds(k * 2, 2)].reshape(1024, 512), right[...])
            for i in range(2):
                g = k * 2 + i
                wbuf[e, h, pl.ds(g * 4, 4)] = pack(o[i * 512:(i + 1) * 512]).reshape(4, 32, 128)
            for j in (0, 1, 3):
                tcopy(e, h, k * 2, j).start()

            @pl.when(k > 0)
            def _():
                tcopy(e, h, k * 2, OWN).start()

            for j in range(4):
                tcopy(e, h, k * 2 + 1, j).start()

    def gather_products(e, h, n_ref):
        @pl.loop(0, NG // 2)
        def _(k):
            for j in range(8):
                if j != OWN:
                    arrival(e, h, k * 8 + j).wait_recv()

            @pl.when(k > 0)
            def _():
                arrival(e, h, k * 8 + OWN).wait_recv()

            @pl.when(k == 0)
            def _():
                zbuf[e, h, OWN] = wbuf[e, h, OWN]
                acc[...] = jnp.zeros_like(acc)

            a = zbuf[e, h, pl.ds(k * 8, 4)].reshape(128, 128)
            b = zbuf[e, h, pl.ds(k * 8 + 4, 4)].reshape(128, 128)
            acc[...] += dot(n_ref[k * 2], rhs(a, -1.0)) + dot(n_ref[k * 2 + 1], rhs(b, -1.0))

        return pack(acc[...])

    def sent(e, h):
        @pl.loop(0, NTILE)
        def _(p):
            @pl.when(p != OWN)
            def _():
                arrival(e, h, p).wait_send()

    def scopy(n, peer, at):
        return pltpu.make_async_remote_copy(
            src_ref=sc_send.at[n], dst_ref=sc_recv.at[n, at],
            send_sem=ss_sem.at[n, peer], recv_sem=sr_sem.at[n, at],
            device_id={"tile": peer}, device_id_type=MESH)

    def s2copy(n, peer, at):
        return pltpu.make_async_remote_copy(
            src_ref=sc2_send.at[n], dst_ref=sc2_recv.at[n, at],
            send_sem=s2s_sem.at[n, peer], recv_sem=s2r_sem.at[n, at],
            device_id={"freq": peer}, device_id_type=MESH)

    def sum_start(n, gn, im):
        row = lax.broadcasted_iota(jnp.int32, (8, 128), 0)
        inn = sum(jnp.sum(i * i, axis=0, keepdims=True) for i in im)
        sc_send[n] = jnp.where(row == 0, gn, jnp.where(row == 1, inn, 0.0))

        @pl.loop(1, NTILE)
        def _(d):
            scopy(n, lax.rem(me + d, NTILE), me).start()

    def sum_middle(n):
        @pl.loop(1, NTILE)
        def _(d):
            peer = lax.rem(me + d, NTILE)
            scopy(n, peer, peer).wait()

        sc_recv[n, me] = sc_send[n]
        part = jnp.sum(sc_recv[n], axis=0)
        sc2_send[n] = part
        for d in range(1, NF):
            s2copy(n, lax.rem(fme + d, NF), fme).start()

    def sum_end(n):
        for d in range(1, NF):
            peer = lax.rem(fme + d, NF)
            s2copy(n, peer, peer).wait()
        sc2_recv[n, fme] = sc2_send[n]
        both = jnp.sum(jnp.sum(sc2_recv[n], axis=0), axis=1, keepdims=True)
        return both[0:1] / both[1:2]

    def setup_gram():
        @pl.loop(0, BLK)
        def _(r):
            t = lanes((1, NT))
            keep_ref[pl.ds(r, 1), :] = (t >= mute_ref[r]).astype(F32)

        gram = jnp.dot(keep_ref[...], prod_ref[...], precision=lax.Precision.HIGHEST, preferred_element_type=F32)
        lane = lanes((32, 128))
        left, real = lane < 64, even((32, 128))

        def col(a, b):
            i = a * 8 + b
            return jnp.where(left, gram[:32, i:i + 1], gram[32:, i:i + 1])

        for fo in range(NF):
            for fi in range(NF):
                gmap[fo, fi, 0] = jnp.where(real, col(fo, fi), col(4 + fo, 4 + fi))
                gmap[fo, fi, 1] = jnp.where(real, col(fo, 4 + fi), col(4 + fo, fi))

    def mix(e, h, spec):
        swapped = [swap(s) for s in spec]
        total = jnp.zeros((1, 128), F32)
        for fo in range(NF):
            o = jnp.zeros((32, 128), F32)
            for fi in range(NF):
                o += gmap[fo, fi, 0] * spec[fi] + gmap[fo, fi, 1] * swapped[fi]
            fsend[e, h, pl.ds(fo * 32, 32), :] = o
            total += jnp.sum(spec[fo] * o, axis=0, keepdims=True)
        gn_ref[h] = total

    def read_spec(ref):
        return [ref[pl.ds(f * 32, 32), :] for f in range(NF)]

    fsend[0] = spec_ref[...]
    pl.semaphore_wait(bar, NTILE - 1 + NF - 1)
    fstart(0, 0)
    fstart(0, 1)

    flat = jnp.concatenate([data_ref[c, h * 32:(h + 1) * 32, :] for h in range(2) for c in range(2)], 0).T
    for b in range(4):
        first, second = flat[b * 64:b * 64 + 32], flat[b * 64 + 32:b * 64 + 64]
        left = lanes((32, 128)) < 64
        r0_ref[0, b * 32:(b + 1) * 32, :] = jnp.where(left, first, pltpu.roll(second, 64, 1))
        r0_ref[1, b * 32:(b + 1) * 32, :] = jnp.where(left, pltpu.roll(first, 64, 1), second)

    loads[0].wait()

    @pl.loop(0, 2)
    def _(h):
        fwait(0, h)
        send_products(0, h, vt, frecv[0, h])

    loads[1].wait()
    setup_wide(ut, un)

    @pl.loop(0, 2)
    def _(h):
        r0_ref[h] = gather_products(0, h, un) - r0_ref[h]
        send_products(1, h, ut, r0_ref[h])

    setup_wide(vt, vn)
    setup_gram()

    @pl.loop(0, 2)
    def _(h):
        fsend[1, h] = gather_products(1, h, vn)
        fstart(1, h)

    @pl.loop(0, 2)
    def _(h):
        fwait(1, h)
        spec0[h] = frecv[1, h]
        mix(2, h, read_spec(spec0.at[h]))
        fstart(2, h)

    @pl.loop(0, 2)
    def _(h):
        fwait(2, h)
        send_products(2, h, vt, frecv[2, h])

    @pl.loop(0, 2)
    def _(h):
        im_ref[h] = gather_products(2, h, un)
        send_products(3, h, ut, im_ref[h])

    sum_start(0, gn_ref[0] + gn_ref[1], (im_ref[0], im_ref[1]))
    fsend[3, 0] = gather_products(3, 0, vn)
    fstart(3, 0)
    sum_middle(0)
    fsend[3, 1] = gather_products(3, 1, vn)
    fstart(3, 1)
    alpha0 = sum_end(0)

    @pl.loop(0, 2)
    def _(h):
        fwait(3, h)
        comb_ref[h] = spec0[h] - alpha0 * frecv[3, h]
        mix(4, h, read_spec(comb_ref.at[h]))
        fstart(4, h)

    @pl.loop(0, 2)
    def _(h):
        fwait(4, h)
        send_products(4, h, vt, frecv[4, h])

    for h in range(2):
        r0_ref[h] = r0_ref[h] - alpha0 * im_ref[h]

    @pl.loop(0, 2)
    def _(h):
        im_ref[h] = gather_products(4, h, un)

    sum_start(1, gn_ref[0] + gn_ref[1], (im_ref[0], im_ref[1]))

    @pl.loop(0, 5)
    def _(e):
        for h in range(2):
            sent(e, h)

    sum_middle(1)
    alpha1 = sum_end(1)
    for h in range(2):
        comb_ref[h] = alpha0 * spec0[h] + alpha1 * comb_ref[h]
    blocks = []
    p0, p1 = (r0_ref[h] - alpha1 * im_ref[h] for h in range(2))
    for b in range(4):
        left = lanes((32, 128)) < 64
        a0, a1 = p0[b * 32:(b + 1) * 32], p1[b * 32:(b + 1) * 32]
        blocks.append(jnp.where(left, a0, pltpu.roll(a1, 64, 1)))
        blocks.append(jnp.where(left, pltpu.roll(a0, 64, 1), a1))
    flat = jnp.concatenate(blocks, 0).T
    for h in range(2):
        for c in range(2):
            resid_ref[c, h * 32:(h + 1) * 32, :] = flat[(h * 2 + c) * 32:(h * 2 + c + 1) * 32]


def update_kernel(mute_ref, comb_ref, b3_ref, x_ref, o_ref):
    g = pl.program_id(0)
    n = x_ref.shape[1]
    b3 = b3_ref[...]
    t = lanes((NV, NT))
    quarter = even((4, 128))
    for i in range(n):
        m = g * n + i
        p0, p1 = (comb_ref[h, pl.ds(m, 4, stride=32), :] for h in range(2))
        re = jnp.where(quarter, p0, pltpu.roll(p1, 32, 1))
        im = jnp.where(quarter, pltpu.roll(p0, 96, 1), p1)
        hi, lo = split(jnp.concatenate([re, im], 0))
        hi, lo = hi.astype(F32), lo.astype(F32)
        lhs = jnp.concatenate([hi, lo, hi, jnp.zeros_like(hi)], 0)
        grad = dot(lhs.T.astype(BF16), b3)
        for s in range(2):
            part = jnp.where(t >= mute_ref[s * 32 + m], grad[s * 64:(s + 1) * 64], 0.0)
            o_ref[s, i] = x_ref[s, i] - part


def body(x_time, mute, ranks, right_factor_columns, u_rows, data):
    b = basis()
    bhi, blo = split(jnp.asarray(b))
    bb = jnp.concatenate([bhi, blo], 0)
    b3 = jnp.concatenate([bhi, bhi, blo, jnp.zeros_like(bhi)], 0)
    prod = np.zeros((NT, 128), np.float32)
    prod[:, :64] = (b[:, None, :] * b[None, :, :]).reshape(64, NT).T
    me = lax.axis_index("tile")
    place = np.array([(*(FIRST, SECOND)[j // 2][g], j % 2) for g in range(NG) for j in range(4)], np.int32)
    perm = (me // 8 + place[:, 0]) % 4 * 8 + (me // 2 % 4 + place[:, 1]) % 4 * 2 + (me % 2 + place[:, 2]) % 2
    vmem = pl.BlockSpec(memory_space=pltpu.VMEM)
    hbm = pl.BlockSpec(memory_space=pl.ANY)
    smem = pl.BlockSpec(memory_space=pltpu.SMEM)
    dma = pltpu.SemaphoreType.DMA
    tiles = jax.ShapeDtypeStruct((NG, 512, 512), BF16)
    spec, vt, ut = pl.pallas_call(
        setup_kernel,
        out_shape=(jax.ShapeDtypeStruct((2, 128, 128), F32), tiles, tiles),
        in_specs=[smem, smem, smem, hbm, hbm, hbm, vmem],
        out_specs=(vmem, hbm, hbm),
        scratch_shapes=[
            pltpu.VMEM((4096, 256), F32),
            pltpu.VMEM((2, 2, 256, NTILE * 64), F32),
            pltpu.VMEM((2, 2, NTILE * 64, 128), F32),
            pltpu.VMEM((2, NG, 512, 512), BF16),
            pltpu.SMEM((2, NTILE), jnp.int32),
            dma((5,)), dma((2, NG)),
        ],
        compiler_params=pltpu.CompilerParams(vmem_limit_bytes=ROOM),
        name="setup",
    )(me.reshape(1), perm.astype(jnp.int32), ranks[0], x_time.reshape(4096, 256), right_factor_columns[0, :, 0], u_rows[0, :, 0], bb)
    pairs = (2, 128, 128)
    comb, resid = pl.pallas_call(
        main_kernel,
        out_shape=(jax.ShapeDtypeStruct(pairs, F32), jax.ShapeDtypeStruct((2, NV, NB), F32)),
        in_specs=[smem, vmem, hbm, hbm, vmem, vmem],
        out_specs=(vmem, vmem),
        scratch_shapes=[
            pltpu.VMEM((NG, 512, 512), BF16),
            pltpu.VMEM((NG, 512, 512), BF16),
            pltpu.VMEM((NG, 512, 512), BF16),
            pltpu.VMEM((NG, 512, 512), BF16),
            pltpu.VMEM((5, 2, NTILE, 32, 128), F32),
            pltpu.VMEM((5, 2, NTILE, 32, 128), F32),
            pltpu.VMEM((5, *pairs), F32),
            pltpu.VMEM((5, *pairs), F32),
            pltpu.VMEM(pairs, F32),
            pltpu.VMEM((512, 128), BF16),
            pltpu.VMEM((512, 128), F32),
            pltpu.VMEM((BLK, NT), F32),
            pltpu.VMEM((NF, NF, 2, 32, 128), F32),
            pltpu.VMEM(pairs, F32),
            pltpu.VMEM(pairs, F32),
            pltpu.VMEM((2, 1, 128), F32),
            pltpu.VMEM((2, 8, 128), F32),
            pltpu.VMEM((2, NTILE, 8, 128), F32),
            pltpu.VMEM((2, 8, 128), F32),
            pltpu.VMEM((2, NF, 8, 128), F32),
            dma((2,)), dma((5, 2, NTILE)), dma((5, 2, NTILE)), dma((5, 2, NF)), dma((5, 2, NF)),
            dma((2, NTILE)), dma((2, NTILE)), dma((2, NF)), dma((2, NF)),
        ],
        compiler_params=pltpu.CompilerParams(collective_id=0, has_side_effects=True, vmem_limit_bytes=ROOM),
        name="descent",
    )(mute, spec, vt, ut, data[0].swapaxes(1, 2), jnp.asarray(prod))
    step = 8
    x_out = pl.pallas_call(
        update_kernel,
        grid=(32 // step,),
        out_shape=jax.ShapeDtypeStruct((2, 32, NV, NT), F32),
        in_specs=[
            smem, vmem, vmem,
            pl.BlockSpec((2, step, NV, NT), lambda i: (0, i, 0, 0)),
        ],
        out_specs=pl.BlockSpec((2, step, NV, NT), lambda i: (0, i, 0, 0)),
        compiler_params=pltpu.CompilerParams(vmem_limit_bytes=ROOM),
        name="update",
    )(mute, comb, b3, x_time.reshape(2, 32, NV, NT))
    return x_out.reshape(BLK, NV, NT), resid.swapaxes(1, 2)[None]


def solution(mesh):
    in_specs = (
        P(("tile", "freq"), None, None),
        P(("tile", "freq")),
        P("freq", None, None),
        P("freq", None, "tile", None, None),
        P("freq", None, "tile", None, None),
        P("freq", None, "tile", None),
    )
    out_specs = (P(("tile", "freq"), None, None), P("freq", None, "tile", None))
    return jax.shard_map(body, mesh=mesh, in_specs=in_specs, out_specs=out_specs, check_vma=False)
```

time: 162 us -> 143 us (0.88)
  local copies, waits for them, and re-layouts: 16.1 us -> 0.66 us
  Pallas kernels: 145 us -> 140 us
    unnamed x22 -> x3, local copies, waits for them, and re-layouts: 14.8 us -> 0.66 us
    pallas_call x3, Pallas kernels: 145 us -> 140 us  [the longest x1 117 us: body(): pl.pallas_call(main_kernel, out_shape=(jax.ShapeDtypeStruct(pairs, F32),...]
where the time goes in v2:
time: 143 us
  Pallas kernels  140 us (98%)
    pallas_call x1, Pallas kernels, body(): pl.pallas_call(main_kernel, out_shape=(jax.ShapeDtypeStruct(pairs, F32),...  117 us
    pallas_call x1, Pallas kernels, body(): pl.pallas_call(setup_kernel, out_shape=(jax.ShapeDtypeStruct((2, 128, 128...  17.3 us
    pallas_call x1, Pallas kernels, body(): pl.pallas_call(update_kernel, grid=(32 // step,), out_shape=jax.ShapeDtyp...  5.69 us

profile of v2, /device:TPU:1, one launch (start us, length us, event | category | flops | bytes accessed | tf_op | source)
XLA Modules:
  0.0 142.7 jit_solution(15561082569989636585)
XLA Ops:
  0.7 1.2 fusion.perm_ref
  1.9 17.3 %setup.1 = (f32[2,128,128]{2,1,0:T(8,128)}, bf16[8,512,512]{2,1,0:T(8,128)(2,1)}, bf16[8,512,512]{2,1,0:T(8,128)(2,1)}) custom-call(s32[1]{0:T(128)} %bitcast.me_ref, s32[32]{0:T(128)} %fusion.perm_ref, s32[32,32]{1,0:T(8,128)} %bitcast.20, f32[4096,256]{1,0:T(8,128)} %bitcast.13, f32[2,256,2048]{2,1,0:T(8,128)} %bitcast.15, f32[2,256,2048]{2,1,0:T(8,128)} %bitcast.16, ...), custom_call_target="tpu_custom_call" | custom-call | tf_op jit(solution)/shard_map/setup/pallas_call | solution.py:479
  19.2 117.1 %descent.1 = (f32[2,128,128]{2,1,0:T(8,128)}, f32[2,64,256]{2,1,0:T(8,128)}) custom-call(s32[64]{0:T(128)} %mute_ref.3, f32[2,128,128]{2,1,0:T(8,128)} %get-tuple-element.7.spec_ref, bf16[8,512,512]{2,1,0:T(8,128)(2,1)} %get-tuple-element.8.vt_hbm, bf16[8,512,512]{2,1,0:T(8,128)(2,1)} %get-tuple-element.9.ut_hbm, f32[2,64,256]{2,1,0:T(8,128)} %bitcast.18, ...), custom_call_target="tpu_custom_call" | custom-call | tf_op jit(solution)/shard_map/descent/pallas_call | solution.py:496
  136.3 0.0 copy-start
  136.3 5.7 %update.1 = f32[2,32,64,256]{3,2,1,0:T(8,128)} custom-call(s32[64]{0:T(128)} %mute_ref.3, f32[2,128,128]{2,1,0:T(8,128)} %get-tuple-element.10.comb_ref, bf16[32,256]{1,0:T(8,128)(2,1)} %constant.97.b3_ref, f32[2,32,64,256]{3,2,1,0:T(8,128)} %bitcast.14), custom_call_target="tpu_custom_call" | custom-call | tf_op jit(solution)/shard_map/update/pallas_call | solution.py:529
  142.0 0.0 copy-done
  142.0 0.7 copy.14
Async XLA Ops:
  136.3 5.7 %copy-start = (f32[2,64,256]{2,1,0:T(8,128)S(1)}, f32[2,64,256]{2,1,0:T(8,128)}, u32[]{:S(2)}) copy-start(f32[2,64,256]{2,1,0:T(8,128)} %get-tuple-element.11) | copy-start | bytes 393220

commit v3 on v2

v3 whole, which is shorter than its diff:
```python
import jax
import jax.numpy as jnp
import numpy as np
from jax import lax
from jax.experimental import pallas as pl
from jax.experimental.pallas import tpu as pltpu
from jax.sharding import PartitionSpec as P

FLO = 16
MESH = pl.DeviceIdType.MESH
F32, BF16 = jnp.float32, jnp.bfloat16
NF, NTILE, NB, NV, NT, BLK = 4, 32, 256, 64, 256, 64
NG = 8
STEP = 4
ROOM = 60 << 20

FIRST = ((0, 0), (2, 1), (1, 2), (1, 1), (1, 3), (2, 0), (1, 0), (0, 1))
SECOND = ((2, 2), (2, 3), (3, 2), (3, 3), (3, 1), (0, 2), (3, 0), (0, 3))
OWN = 0


def basis():
    steps = np.arange(NT)
    freqs = FLO + np.arange(NF)
    angle = (freqs[:, None] * steps[None, :] % NT).astype(np.float32) * np.float32(2.0 * np.pi / NT)
    return np.concatenate([np.cos(angle), -np.sin(angle)]).astype(np.float32)


def split(a):
    hi = a.astype(BF16)
    return hi, (a - hi.astype(F32)).astype(BF16)


def dot(a, b, dims=((1,), (0,))):
    return lax.dot_general(a, b, (dims, ((), ())), preferred_element_type=F32)


def lanes(shape):
    return lax.broadcasted_iota(jnp.int32, shape, 1)


def even(shape):
    return lax.rem(lanes(shape), 64) < 32


def swap(p):
    return jnp.where(even(p.shape), pltpu.roll(p, 96, 1), pltpu.roll(p, 32, 1))


def rhs(p, sign):
    left = lanes(p.shape) < 64
    s = swap(p)
    out = []
    for q in (p, jnp.where(even(p.shape), sign * s, -sign * s)):
        hi = q.astype(BF16).astype(F32)
        lo = q - hi
        out.append(jnp.where(left, hi, pltpu.roll(lo, 64, 1)).astype(BF16))
        out.append(jnp.where(left, pltpu.roll(hi, 64, 1), lo).astype(BF16))
    return jnp.concatenate(out, 0)


def pack(o):
    s = o[:256] + o[256:]
    s = s + pltpu.roll(s, 64, 1)
    return jnp.where(lanes((128, 128)) < 64, s[:128], s[128:])


def tile_at(me, g, j):
    table, dc = (FIRST, SECOND)[j // 2], j % 2
    dz, dy = jnp.int32(table[0][0]), jnp.int32(table[0][1])
    for i in range(1, NG):
        dz, dy = jnp.where(g == i, table[i][0], dz), jnp.where(g == i, table[i][1], dy)
    return lax.rem(me // 8 + dz, 4) * 8 + lax.rem(lax.rem(me // 2, 4) + dy, 4) * 2 + lax.rem(lax.rem(me, 2) + dc, 2)


def setup_kernel(ranks_ref, v_hbm, u_hbm, vt_hbm, ut_hbm, raw, tall, packed, offs, ld_sem, st_sem):
    me = lax.axis_index("tile")
    loads = []
    for m, hbm in enumerate((v_hbm, u_hbm)):
        for c in range(2):
            loads.append(pltpu.make_async_copy(hbm.at[c], raw.at[m, c], ld_sem.at[m * 2 + c]))
    for cp in loads:
        cp.start()

    def offsets(m, rank_at):
        def one(i, off):
            offs[m, i] = off
            return off + rank_at(i)

        lax.fori_loop(0, NTILE, one, jnp.int32(0))

    ranks_at = (lambda i: ranks_ref[i, me]), (lambda j: ranks_ref[me, j])
    offsets(0, ranks_at[0])
    offsets(1, ranks_at[1])

    def flip(m):
        for c in range(2):
            loads[m * 2 + c].wait()

            @pl.loop(0, 16)
            def _(b):
                cols = pl.ds(pl.multiple_of(b * 128, 128), 128)
                order = [64 * i for i in range(4)] + [64 * i + 32 for i in range(4)]
                turned = jnp.concatenate([raw[m, c, i:i + 32, cols] for i in order], 0).T
                tall[c, 0, cols, :] = turned[:, :128]
                tall[c, 1, cols, :] = turned[:, 128:]

    def store(m, g):
        return pltpu.make_async_copy(packed.at[m, g], (vt_hbm, ut_hbm)[m].at[g], st_sem.at[m, g])

    def pad(m):
        @pl.loop(0, NG)
        def _(g):
            for j in range(4):
                tile = tile_at(me, g, j)
                k = ranks_at[m](tile)
                off = offs[m, tile]
                for c in range(2):
                    piece = jnp.concatenate([tall[c, h, pl.ds(off, 64), :] for h in range(2)], 1)
                    slot = lax.broadcasted_iota(jnp.int32, (64, NB), 0)
                    for n, part in enumerate(split(jnp.where(slot < k, piece, 0.0))):
                        for h in range(2):
                            at = n * 256 + h * 128 + j * 32
                            packed[m, g, at:at + 32, c * 256:(c + 1) * 256] = part[h * 32:(h + 1) * 32]
            store(m, g).start()

    for m in range(2):
        flip(m)
        pad(m)
    for m in range(2):
        @pl.loop(0, NG)
        def _(g):
            store(m, g).wait()


def main_kernel(
    mute_ref, x_hbm, vt_hbm, ut_hbm, data_ref, bb_ref, prod_ref,
    comb_ref, resid_ref,
    x_buf, vt, vn, ut, un, wbuf, zbuf, fsend, frecv, spec0, right, acc,
    keep_ref, gmap, r0_ref, im_ref, gn_ref, sc_send, sc_recv, sc2_send, sc2_recv,
    ld_sem, ts_sem, tr_sem, fs_sem, fr_sem, ss_sem, sr_sem, s2s_sem, s2r_sem,
):
    me = lax.axis_index("tile")
    fme = lax.axis_index("freq")

    loads = [
        pltpu.make_async_copy(x_hbm, x_buf, ld_sem.at[2]),
        pltpu.make_async_copy(vt_hbm, vt, ld_sem.at[0]),
        pltpu.make_async_copy(ut_hbm, ut, ld_sem.at[1]),
    ]
    for cp in loads:
        cp.start()

    bar = pltpu.get_barrier_semaphore()

    @pl.loop(1, NTILE)
    def _(d):
        pl.semaphore_signal(bar, inc=1, device_id={"tile": lax.rem(me + d, NTILE)}, device_id_type=MESH)

    for d in range(1, NF):
        pl.semaphore_signal(bar, inc=1, device_id={"freq": lax.rem(fme + d, NF)}, device_id_type=MESH)

    def setup_wide(t_ref, n_ref):
        @pl.loop(0, NG)
        def _(g):
            for p in range(2):
                for c in range(2):
                    n_ref[g, p * 256:(p + 1) * 256, c * 256:(c + 1) * 256] = (
                        t_ref[g, p * 256:(p + 1) * 256, c * 256:(c + 1) * 256].T)

    def fcopy(e, h, peer, at):
        return pltpu.make_async_remote_copy(
            src_ref=fsend.at[e, h, pl.ds(pl.multiple_of(peer * 32, 32), 32)],
            dst_ref=frecv.at[e, h, pl.ds(pl.multiple_of(at * 32, 32), 32)],
            send_sem=fs_sem.at[e, h, peer], recv_sem=fr_sem.at[e, h, at],
            device_id={"freq": peer}, device_id_type=MESH)

    def fstart(e, h):
        for d in (2, 1, 3):
            fcopy(e, h, lax.rem(fme + d, NF), fme).start()

    def fwait(e, h):
        for d in range(1, NF):
            peer = lax.rem(fme + d, NF)
            fcopy(e, h, peer, peer).wait()
        own = pl.ds(pl.multiple_of(fme * 32, 32), 32)
        frecv[e, h, own, :] = fsend[e, h, own, :]

    def tcopy(e, h, g, j):
        half, dc = j // 2, j % 2
        peer = tile_at(me, g, j)
        same = jnp.logical_or(g == 0, g == 5)
        slot = g * 4 + jnp.where(same, half, 1 - half) * 2 + dc
        return pltpu.make_async_remote_copy(
            src_ref=wbuf.at[e, h, g * 4 + j], dst_ref=zbuf.at[e, h, slot],
            send_sem=ts_sem.at[e, h], recv_sem=tr_sem.at[e, h, g // STEP],
            device_id={"tile": peer}, device_id_type=MESH)

    def arrivals(e, h, k):
        slots = pl.ds(max(k * STEP * 4, 1), STEP * 4 - (k == 0))
        return pltpu.make_async_remote_copy(
            src_ref=wbuf.at[e, h, slots], dst_ref=zbuf.at[e, h, slots],
            send_sem=ts_sem.at[e, h], recv_sem=tr_sem.at[e, h, k],
            device_id={"tile": lax.rem(me + 1, NTILE)}, device_id_type=MESH)

    def send_products(e, h, t_ref, p, sign=1.0):
        right[...] = rhs(p, sign)

        @pl.loop(0, NG // STEP)
        def _(k):
            o = dot(t_ref[pl.ds(k * STEP, STEP)].reshape(STEP * 512, 512), right[...])
            for i in range(STEP):
                wbuf[e, h, pl.ds((k * STEP + i) * 4, 4)] = pack(o[i * 512:(i + 1) * 512]).reshape(4, 32, 128)
            for i in range(STEP):
                for j in range(4):
                    if i or j != OWN:
                        tcopy(e, h, k * STEP + i, j).start()
                    else:
                        @pl.when(k > 0)
                        def _():
                            tcopy(e, h, k * STEP, OWN).start()

    def gather_part(e, h, n_ref, k):
        arrivals(e, h, k).wait_recv()
        if k == 0:
            zbuf[e, h, OWN] = wbuf[e, h, OWN]
        total = None
        for g in range(k * STEP, (k + 1) * STEP):
            z = zbuf[e, h, g * 4:g * 4 + 4].reshape(128, 128)
            o = dot(n_ref[g], rhs(z, -1.0))
            total = o if total is None else total + o
        if k == 0:
            acc[...] = total
        else:
            acc[...] += total

    def gather_products(e, h, n_ref):
        for k in range(NG // STEP):
            gather_part(e, h, n_ref, k)
        return pack(acc[...])

    def sent(e, h):
        slots = pl.ds(1, NTILE - 1)
        pltpu.make_async_remote_copy(
            src_ref=wbuf.at[e, h, slots], dst_ref=zbuf.at[e, h, slots],
            send_sem=ts_sem.at[e, h], recv_sem=tr_sem.at[e, h, 0],
            device_id={"tile": lax.rem(me + 1, NTILE)}, device_id_type=MESH).wait_send()

    def scopy(n, d):
        return pltpu.make_async_remote_copy(
            src_ref=sc_send.at[n], dst_ref=sc_recv.at[n, d],
            send_sem=ss_sem.at[n], recv_sem=sr_sem.at[n],
            device_id={"tile": lax.rem(me + d, NTILE)}, device_id_type=MESH)

    def s2copy(n, peer, at):
        return pltpu.make_async_remote_copy(
            src_ref=sc2_send.at[n], dst_ref=sc2_recv.at[n, at],
            send_sem=s2s_sem.at[n, peer], recv_sem=s2r_sem.at[n, at],
            device_id={"freq": peer}, device_id_type=MESH)

    def sum_start(n, gn, im):
        row = lax.broadcasted_iota(jnp.int32, (8, 128), 0)
        inn = sum(jnp.sum(i * i, axis=0, keepdims=True) for i in im)
        sc_send[n] = jnp.where(row == 0, gn, jnp.where(row == 1, inn, 0.0))

        @pl.loop(1, NTILE)
        def _(d):
            scopy(n, d).start()

    def sum_middle(n):
        rest = sc_recv.at[n, pl.ds(1, NTILE - 1)]
        pltpu.make_async_remote_copy(
            src_ref=rest, dst_ref=rest, send_sem=ss_sem.at[n], recv_sem=sr_sem.at[n],
            device_id={"tile": lax.rem(me + 1, NTILE)}, device_id_type=MESH).wait()
        sc_recv[n, 0] = sc_send[n]
        part = jnp.sum(sc_recv[n], axis=0)
        sc2_send[n] = part
        for d in range(1, NF):
            s2copy(n, lax.rem(fme + d, NF), fme).start()

    def sum_end(n):
        for d in range(1, NF):
            peer = lax.rem(fme + d, NF)
            s2copy(n, peer, peer).wait()
        sc2_recv[n, fme] = sc2_send[n]
        both = jnp.sum(jnp.sum(sc2_recv[n], axis=0), axis=1, keepdims=True)
        return both[0:1] / both[1:2]

    def setup_gram():
        @pl.loop(0, BLK)
        def _(r):
            t = lanes((1, NT))
            keep_ref[pl.ds(r, 1), :] = (t >= mute_ref[r]).astype(F32)

        gram = jnp.dot(keep_ref[...], prod_ref[...], precision=lax.Precision.HIGHEST, preferred_element_type=F32)
        lane = lanes((32, 128))
        left, real = lane < 64, even((32, 128))

        def col(a, b):
            i = a * 8 + b
            return jnp.where(left, gram[:32, i:i + 1], gram[32:, i:i + 1])

        for fo in range(NF):
            for fi in range(NF):
                gmap[fo, fi, 0] = jnp.where(real, col(fo, fi), col(4 + fo, 4 + fi))
                gmap[fo, fi, 1] = jnp.where(real, col(fo, 4 + fi), col(4 + fo, fi))

    def mix(e, h, spec):
        swapped = [swap(s) for s in spec]
        total = jnp.zeros((1, 128), F32)
        for fo in range(NF):
            o = jnp.zeros((32, 128), F32)
            for fi in range(NF):
                o += gmap[fo, fi, 0] * spec[fi] + gmap[fo, fi, 1] * swapped[fi]
            fsend[e, h, pl.ds(fo * 32, 32), :] = o
            total += jnp.sum(spec[fo] * o, axis=0, keepdims=True)
        gn_ref[h] = total

    def read_spec(ref):
        return [ref[pl.ds(f * 32, 32), :] for f in range(NF)]

    loads[0].wait()
    bb = bb_ref[...]
    quarter = even((4, 128))

    @pl.loop(0, BLK // 4)
    def _(k):
        low = pl.multiple_of(k * 128, 128)
        a, b = x_buf[pl.ds(low, 128), :], x_buf[pl.ds(BLK * 32 + low, 128), :]
        hi, lo = split(jnp.concatenate([a[:64], b[:64], a[64:], b[64:]], 0))
        o1 = dot(bb, hi, ((1,), (1,)))
        o2 = dot(bb, lo, ((1,), (1,)))
        o = o1[:8] + o1[8:] + o2[:8]
        for i in range(2):
            re, im = o[:4, i * 128:(i + 1) * 128], o[4:, i * 128:(i + 1) * 128]
            rows = pl.ds(k * 2 + i, 4, stride=32)
            fsend[0, 0, rows, :] = jnp.where(quarter, re, pltpu.roll(im, 32, 1))
            fsend[0, 1, rows, :] = jnp.where(quarter, pltpu.roll(re, 96, 1), im)

    pl.semaphore_wait(bar, NTILE - 1 + NF - 1)
    fstart(0, 0)
    fstart(0, 1)

    flat = jnp.concatenate([data_ref[c, h * 32:(h + 1) * 32, :] for h in range(2) for c in range(2)], 0).T
    for b in range(4):
        first, second = flat[b * 64:b * 64 + 32], flat[b * 64 + 32:b * 64 + 64]
        left = lanes((32, 128)) < 64
        r0_ref[0, b * 32:(b + 1) * 32, :] = jnp.where(left, first, pltpu.roll(second, 64, 1))
        r0_ref[1, b * 32:(b + 1) * 32, :] = jnp.where(left, pltpu.roll(first, 64, 1), second)

    loads[1].wait()

    @pl.loop(0, 2)
    def _(h):
        fwait(0, h)
        send_products(0, h, vt, frecv[0, h])

    loads[2].wait()
    setup_wide(ut, un)

    @pl.loop(0, 2)
    def _(h):
        r0_ref[h] = gather_products(0, h, un) - r0_ref[h]
        send_products(1, h, ut, r0_ref[h])

    setup_wide(vt, vn)
    setup_gram()

    def adjoint_and_back(e, use, alpha):
        k = NG // STEP - 1
        fsend[e, 0] = gather_products(e, 0, vn)
        fstart(e, 0)
        for i in range(k):
            gather_part(e, 1, vn, i)
        a = alpha()
        fwait(e, 0)
        use(0, a)
        fstart(e + 1, 0)
        gather_part(e, 1, vn, k)
        fsend[e, 1] = pack(acc[...])
        fstart(e, 1)
        fwait(e + 1, 0)
        send_products(e + 1, 0, vt, frecv[e + 1, 0])
        fwait(e, 1)
        use(1, a)
        fstart(e + 1, 1)
        fwait(e + 1, 1)
        send_products(e + 1, 1, vt, frecv[e + 1, 1])
        return a

    def first_use(h, a):
        spec0[h] = frecv[1, h]
        mix(2, h, read_spec(spec0.at[h]))

    adjoint_and_back(1, first_use, lambda: None)

    im_ref[0] = gather_products(2, 0, un)
    send_products(3, 0, ut, im_ref[0])
    im_ref[1] = gather_products(2, 1, un)
    sum_start(0, gn_ref[0] + gn_ref[1], (im_ref[0], im_ref[1]))
    send_products(3, 1, ut, im_ref[1])
    sum_middle(0)

    def second_use(h, a):
        comb_ref[h] = spec0[h] - a * frecv[3, h]
        mix(4, h, read_spec(comb_ref.at[h]))

    alpha0 = adjoint_and_back(3, second_use, lambda: sum_end(0))

    for h in range(2):
        r0_ref[h] = r0_ref[h] - alpha0 * im_ref[h]

    @pl.loop(0, 2)
    def _(h):
        im_ref[h] = gather_products(4, h, un)

    sum_start(1, gn_ref[0] + gn_ref[1], (im_ref[0], im_ref[1]))

    @pl.loop(0, 5)
    def _(e):
        for h in range(2):
            sent(e, h)

    sum_middle(1)
    alpha1 = sum_end(1)
    for h in range(2):
        comb_ref[h] = alpha0 * spec0[h] + alpha1 * comb_ref[h]
    blocks = []
    p0, p1 = (r0_ref[h] - alpha1 * im_ref[h] for h in range(2))
    for b in range(4):
        left = lanes((32, 128)) < 64
        a0, a1 = p0[b * 32:(b + 1) * 32], p1[b * 32:(b + 1) * 32]
        blocks.append(jnp.where(left, a0, pltpu.roll(a1, 64, 1)))
        blocks.append(jnp.where(left, pltpu.roll(a0, 64, 1), a1))
    flat = jnp.concatenate(blocks, 0).T
    for h in range(2):
        for c in range(2):
            resid_ref[c, h * 32:(h + 1) * 32, :] = flat[(h * 2 + c) * 32:(h * 2 + c + 1) * 32]


def update_kernel(mute_ref, comb_ref, b3_ref, x_ref, o_ref):
    g = pl.program_id(0)
    n = x_ref.shape[1]
    b3 = b3_ref[...]
    t = lanes((NV, NT))
    quarter = even((4, 128))
    for i in range(n):
        m = g * n + i
        p0, p1 = (comb_ref[h, pl.ds(m, 4, stride=32), :] for h in range(2))
        re = jnp.where(quarter, p0, pltpu.roll(p1, 32, 1))
        im = jnp.where(quarter, pltpu.roll(p0, 96, 1), p1)
        hi, lo = split(jnp.concatenate([re, im], 0))
        hi, lo = hi.astype(F32), lo.astype(F32)
        lhs = jnp.concatenate([hi, lo, hi, jnp.zeros_like(hi)], 0)
        grad = dot(lhs.T.astype(BF16), b3)
        for s in range(2):
            part = jnp.where(t >= mute_ref[s * 32 + m], grad[s * 64:(s + 1) * 64], 0.0)
            o_ref[s, i] = x_ref[s, i] - part


def body(x_time, mute, ranks, right_factor_columns, u_rows, data):
    b = basis()
    bhi, blo = split(jnp.asarray(b))
    bb = jnp.concatenate([bhi, blo], 0)
    b3 = jnp.concatenate([bhi, bhi, blo, jnp.zeros_like(bhi)], 0)
    prod = np.zeros((NT, 128), np.float32)
    prod[:, :64] = (b[:, None, :] * b[None, :, :]).reshape(64, NT).T
    vmem = pl.BlockSpec(memory_space=pltpu.VMEM)
    hbm = pl.BlockSpec(memory_space=pl.ANY)
    smem = pl.BlockSpec(memory_space=pltpu.SMEM)
    dma = pltpu.SemaphoreType.DMA
    tiles = jax.ShapeDtypeStruct((NG, 512, 512), BF16)
    vt, ut = pl.pallas_call(
        setup_kernel,
        out_shape=(tiles, tiles),
        in_specs=[smem, hbm, hbm],
        out_specs=(hbm, hbm),
        scratch_shapes=[
            pltpu.VMEM((2, 2, 256, NTILE * 64), F32),
            pltpu.VMEM((2, 2, NTILE * 64, 128), F32),
            pltpu.VMEM((2, NG, 512, 512), BF16),
            pltpu.SMEM((2, NTILE), jnp.int32),
            dma((4,)), dma((2, NG)),
        ],
        compiler_params=pltpu.CompilerParams(vmem_limit_bytes=ROOM),
        name="setup",
    )(ranks[0], right_factor_columns[0, :, 0], u_rows[0, :, 0])
    pairs = (2, 128, 128)
    comb, resid = pl.pallas_call(
        main_kernel,
        out_shape=(jax.ShapeDtypeStruct(pairs, F32), jax.ShapeDtypeStruct((2, NV, NB), F32)),
        in_specs=[smem, hbm, hbm, hbm, vmem, vmem, vmem],
        out_specs=(vmem, vmem),
        scratch_shapes=[
            pltpu.VMEM((4096, 256), F32),
            pltpu.VMEM((NG, 512, 512), BF16),
            pltpu.VMEM((NG, 512, 512), BF16),
            pltpu.VMEM((NG, 512, 512), BF16),
            pltpu.VMEM((NG, 512, 512), BF16),
            pltpu.VMEM((5, 2, NTILE, 32, 128), F32),
            pltpu.VMEM((5, 2, NTILE, 32, 128), F32),
            pltpu.VMEM((5, *pairs), F32),
            pltpu.VMEM((5, *pairs), F32),
            pltpu.VMEM(pairs, F32),
            pltpu.VMEM((512, 128), BF16),
            pltpu.VMEM((512, 128), F32),
            pltpu.VMEM((BLK, NT), F32),
            pltpu.VMEM((NF, NF, 2, 32, 128), F32),
            pltpu.VMEM(pairs, F32),
            pltpu.VMEM(pairs, F32),
            pltpu.VMEM((2, 1, 128), F32),
            pltpu.VMEM((2, 8, 128), F32),
            pltpu.VMEM((2, NTILE, 8, 128), F32),
            pltpu.VMEM((2, 8, 128), F32),
            pltpu.VMEM((2, NF, 8, 128), F32),
            dma((3,)), dma((5, 2)), dma((5, 2, NG // STEP)), dma((5, 2, NF)), dma((5, 2, NF)),
            dma((2,)), dma((2,)), dma((2, NF)), dma((2, NF)),
        ],
        compiler_params=pltpu.CompilerParams(collective_id=0, has_side_effects=True, vmem_limit_bytes=ROOM),
        name="descent",
    )(mute, x_time.reshape(4096, 256), vt, ut, data[0].swapaxes(1, 2), bb, jnp.asarray(prod))
    step = 16
    x_out = pl.pallas_call(
        update_kernel,
        grid=(32 // step,),
        out_shape=jax.ShapeDtypeStruct((2, 32, NV, NT), F32),
        in_specs=[
            smem, vmem, vmem,
            pl.BlockSpec((2, step, NV, NT), lambda i: (0, i, 0, 0)),
        ],
        out_specs=pl.BlockSpec((2, step, NV, NT), lambda i: (0, i, 0, 0)),
        compiler_params=pltpu.CompilerParams(vmem_limit_bytes=ROOM),
        name="update",
    )(mute, comb, b3, x_time.reshape(2, 32, NV, NT))
    return x_out.reshape(BLK, NV, NT), resid.swapaxes(1, 2)[None]


def solution(mesh):
    in_specs = (
        P(("tile", "freq"), None, None),
        P(("tile", "freq")),
        P("freq", None, None),
        P("freq", None, "tile", None, None),
        P("freq", None, "tile", None, None),
        P("freq", None, "tile", None),
    )
    out_specs = (P(("tile", "freq"), None, None), P("freq", None, "tile", None))
    return jax.shard_map(body, mesh=mesh, in_specs=in_specs, out_specs=out_specs, check_vma=False)
```

time: 143 us -> 131 us (0.916)
  Pallas kernels: 140 us -> 130 us
    pallas_call x1, Pallas kernels: 17.3 us -> 12 us  [body(): pl.pallas_call(setup_kernel, out_shape=(tiles, tiles), in_specs=[smem, hb...]
    pallas_call x1, Pallas kernels: 117 us -> 113 us  [body(): pl.pallas_call(main_kernel, out_shape=(jax.ShapeDtypeStruct(pairs, F32),...]
where the time goes in v3:
time: 131 us
  Pallas kernels  130 us (99%)
    pallas_call x1, Pallas kernels, body(): pl.pallas_call(main_kernel, out_shape=(jax.ShapeDtypeStruct(pairs, F32),...  113 us
    pallas_call x1, Pallas kernels, body(): pl.pallas_call(setup_kernel, out_shape=(tiles, tiles), in_specs=[smem, hb...  12 us
    pallas_call x1, Pallas kernels, body(): pl.pallas_call(update_kernel, grid=(32 // step,), out_shape=jax.ShapeDtyp...  4.5 us

profile of v3, /device:TPU:1, one launch (start us, length us, event | category | flops | bytes accessed | tf_op | source)
XLA Modules:
  0.0 131.0 jit_solution(7715585823290227470)
XLA Ops:
  0.6 12.0 %setup.1 = (bf16[8,512,512]{2,1,0:T(8,128)(2,1)}, bf16[8,512,512]{2,1,0:T(8,128)(2,1)}) custom-call(s32[32,32]{1,0:T(8,128)} %bitcast.19, f32[2,256,2048]{2,1,0:T(8,128)} %bitcast.14, f32[2,256,2048]{2,1,0:T(8,128)} %bitcast.15), custom_call_target="tpu_custom_call" | custom-call | tf_op jit(solution)/shard_map/setup/pallas_call | solution.py:473
  12.7 113.1 %descent.1 = (f32[2,128,128]{2,1,0:T(8,128)}, f32[2,64,256]{2,1,0:T(8,128)}) custom-call(s32[64]{0:T(128)} %mute_ref.3, f32[4096,256]{1,0:T(8,128)} %bitcast.12, bf16[8,512,512]{2,1,0:T(8,128)(2,1)} %get-tuple-element.6.vt_hbm, bf16[8,512,512]{2,1,0:T(8,128)(2,1)} %get-tuple-element.7.ut_hbm, f32[2,64,256]{2,1,0:T(8,128)} %bitcast.17, ...), custom_call_target="tpu_custom_call" | custom-call | tf_op jit(solution)/shard_map/descent/pallas_call | solution.py:489
  125.8 0.0 copy-start
  125.8 4.5 %update.1 = f32[2,32,64,256]{3,2,1,0:T(8,128)} custom-call(s32[64]{0:T(128)} %mute_ref.3, f32[2,128,128]{2,1,0:T(8,128)} %get-tuple-element.8.comb_ref, bf16[32,256]{1,0:T(8,128)(2,1)} %constant.19.b3_ref, f32[2,32,64,256]{3,2,1,0:T(8,128)} %bitcast.13), custom_call_target="tpu_custom_call" | custom-call | tf_op jit(solution)/shard_map/update/pallas_call | solution.py:523
  130.3 0.0 copy-done
  130.3 0.7 copy.11
Async XLA Ops:
  125.8 4.5 %copy-start = (f32[2,64,256]{2,1,0:T(8,128)S(1)}, f32[2,64,256]{2,1,0:T(8,128)}, u32[]{:S(2)}) copy-start(f32[2,64,256]{2,1,0:T(8,128)} %get-tuple-element.9) | copy-start | bytes 393220

commit v4 on v3

--- a/solution.py
+++ b/solution.py
@@ -12,6 +12,7 @@
 NF, NTILE, NB, NV, NT, BLK = 4, 32, 256, 64, 256, 64
 NG = 8
 STEP = 4
+NPLANE = NF * (NTILE // 8)
 ROOM = 60 << 20
 
 FIRST = ((0, 0), (2, 1), (1, 2), (1, 1), (1, 3), (2, 0), (1, 0), (0, 1))
@@ -67,9 +68,12 @@
 
 def tile_at(me, g, j):
     table, dc = (FIRST, SECOND)[j // 2], j % 2
-    dz, dy = jnp.int32(table[0][0]), jnp.int32(table[0][1])
-    for i in range(1, NG):
-        dz, dy = jnp.where(g == i, table[i][0], dz), jnp.where(g == i, table[i][1], dy)
+    if isinstance(g, int):
+        dz, dy = table[g]
+    else:
+        dz, dy = jnp.int32(table[0][0]), jnp.int32(table[0][1])
+        for i in range(1, NG):
+            dz, dy = jnp.where(g == i, table[i][0], dz), jnp.where(g == i, table[i][1], dy)
     return lax.rem(me // 8 + dz, 4) * 8 + lax.rem(lax.rem(me // 2, 4) + dy, 4) * 2 + lax.rem(lax.rem(me, 2) + dc, 2)
 
 
@@ -93,40 +97,53 @@
     offsets(0, ranks_at[0])
     offsets(1, ranks_at[1])
 
-    def flip(m):
-        for c in range(2):
-            loads[m * 2 + c].wait()
-
-            @pl.loop(0, 16)
-            def _(b):
-                cols = pl.ds(pl.multiple_of(b * 128, 128), 128)
-                order = [64 * i for i in range(4)] + [64 * i + 32 for i in range(4)]
-                turned = jnp.concatenate([raw[m, c, i:i + 32, cols] for i in order], 0).T
-                tall[c, 0, cols, :] = turned[:, :128]
-                tall[c, 1, cols, :] = turned[:, 128:]
+    order = [64 * i for i in range(4)] + [64 * i + 32 for i in range(4)]
+
+    def flip(m, n):
+        c, cols = n // 16, pl.ds(pl.multiple_of(lax.rem(n, 16) * 128, 128), 128)
+        turned = jnp.concatenate([raw[m, c, i:i + 32, cols] for i in order], 0).T
+        tall[m, c, 0, cols, :] = turned[:, :128]
+        tall[m, c, 1, cols, :] = turned[:, 128:]
 
     def store(m, g):
         return pltpu.make_async_copy(packed.at[m, g], (vt_hbm, ut_hbm)[m].at[g], st_sem.at[m, g])
 
-    def pad(m):
-        @pl.loop(0, NG)
-        def _(g):
-            for j in range(4):
-                tile = tile_at(me, g, j)
-                k = ranks_at[m](tile)
-                off = offs[m, tile]
-                for c in range(2):
-                    piece = jnp.concatenate([tall[c, h, pl.ds(off, 64), :] for h in range(2)], 1)
-                    slot = lax.broadcasted_iota(jnp.int32, (64, NB), 0)
-                    for n, part in enumerate(split(jnp.where(slot < k, piece, 0.0))):
-                        for h in range(2):
-                            at = n * 256 + h * 128 + j * 32
-                            packed[m, g, at:at + 32, c * 256:(c + 1) * 256] = part[h * 32:(h + 1) * 32]
-            store(m, g).start()
-
-    for m in range(2):
-        flip(m)
-        pad(m)
+    def pad(m, g):
+        for j in range(4):
+            tile = tile_at(me, g, j)
+            k = ranks_at[m](tile)
+            off = offs[m, tile]
+            for c in range(2):
+                piece = jnp.concatenate([tall[m, c, h, pl.ds(off, 64), :] for h in range(2)], 1)
+                slot = lax.broadcasted_iota(jnp.int32, (64, NB), 0)
+                for n, part in enumerate(split(jnp.where(slot < k, piece, 0.0))):
+                    for h in range(2):
+                        at = n * 256 + h * 128 + j * 32
+                        packed[m, g, at:at + 32, c * 256:(c + 1) * 256] = part[h * 32:(h + 1) * 32]
+
+    for c in range(2):
+        loads[c].wait()
+
+        @pl.loop(0, NTILE // 4)
+        def _(b):
+            for i in range(2):
+                flip(0, c * 16 + b * 2 + i)
+
+    loads[2].wait()
+    loads[3].wait()
+
+    @pl.loop(0, NG)
+    def _(g):
+        for i in range(4):
+            flip(1, g * 4 + i)
+        pad(0, g)
+        store(0, g).start()
+
+    @pl.loop(0, NG)
+    def _(g):
+        pad(1, g)
+        store(1, g).start()
+
     for m in range(2):
         @pl.loop(0, NG)
         def _(g):
@@ -157,8 +174,16 @@
     def _(d):
         pl.semaphore_signal(bar, inc=1, device_id={"tile": lax.rem(me + d, NTILE)}, device_id_type=MESH)
 
-    for d in range(1, NF):
-        pl.semaphore_signal(bar, inc=1, device_id={"freq": lax.rem(fme + d, NF)}, device_id_type=MESH)
+    def plane_peer(d):
+        w = lax.rem(me // 8 * NF + fme + d, NPLANE)
+        return {"freq": lax.rem(w, NF), "tile": w // NF * 8 + lax.rem(me, 8)}
+
+    met = 0
+    for df in range(1, NF):
+        for dz in range(NTILE // 8):
+            peer = {"freq": lax.rem(fme + df, NF), "tile": lax.rem(me + 8 * dz, NTILE)}
+            pl.semaphore_signal(bar, inc=1, device_id=peer, device_id_type=MESH)
+            met += 1
 
     def setup_wide(t_ref, n_ref):
         @pl.loop(0, NG)
@@ -189,8 +214,7 @@
     def tcopy(e, h, g, j):
         half, dc = j // 2, j % 2
         peer = tile_at(me, g, j)
-        same = jnp.logical_or(g == 0, g == 5)
-        slot = g * 4 + jnp.where(same, half, 1 - half) * 2 + dc
+        slot = g * 4 + (half if g in (0, 5) else 1 - half) * 2 + dc
         return pltpu.make_async_remote_copy(
             src_ref=wbuf.at[e, h, g * 4 + j], dst_ref=zbuf.at[e, h, slot],
             send_sem=ts_sem.at[e, h], recv_sem=tr_sem.at[e, h, g // STEP],
@@ -203,22 +227,20 @@
             send_sem=ts_sem.at[e, h], recv_sem=tr_sem.at[e, h, k],
             device_id={"tile": lax.rem(me + 1, NTILE)}, device_id_type=MESH)
 
-    def send_products(e, h, t_ref, p, sign=1.0):
-        right[...] = rhs(p, sign)
-
-        @pl.loop(0, NG // STEP)
-        def _(k):
-            o = dot(t_ref[pl.ds(k * STEP, STEP)].reshape(STEP * 512, 512), right[...])
-            for i in range(STEP):
-                wbuf[e, h, pl.ds((k * STEP + i) * 4, 4)] = pack(o[i * 512:(i + 1) * 512]).reshape(4, 32, 128)
-            for i in range(STEP):
-                for j in range(4):
-                    if i or j != OWN:
-                        tcopy(e, h, k * STEP + i, j).start()
-                    else:
-                        @pl.when(k > 0)
-                        def _():
-                            tcopy(e, h, k * STEP, OWN).start()
+    def send_part(e, h, t_ref, k):
+        o = dot(t_ref[k * STEP:(k + 1) * STEP].reshape(STEP * 512, 512), right[...])
+        for i in range(STEP):
+            g = k * STEP + i
+            wbuf[e, h, g * 4:g * 4 + 4] = pack(o[i * 512:(i + 1) * 512]).reshape(4, 32, 128)
+        for i in range(STEP):
+            for j in range(4):
+                if k or i or j != OWN:
+                    tcopy(e, h, k * STEP + i, j).start()
+
+    def send_products(e, h, t_ref, p):
+        right[...] = rhs(p, 1.0)
+        for k in range(NG // STEP):
+            send_part(e, h, t_ref, k)
 
     def gather_part(e, h, n_ref, k):
         arrivals(e, h, k).wait_recv()
@@ -250,40 +272,36 @@
         return pltpu.make_async_remote_copy(
             src_ref=sc_send.at[n], dst_ref=sc_recv.at[n, d],
             send_sem=ss_sem.at[n], recv_sem=sr_sem.at[n],
-            device_id={"tile": lax.rem(me + d, NTILE)}, device_id_type=MESH)
-
-    def s2copy(n, peer, at):
+            device_id={"tile": me // 8 * 8 + lax.rem(lax.rem(me, 8) + d, 8)}, device_id_type=MESH)
+
+    def s2copy(n, d):
         return pltpu.make_async_remote_copy(
-            src_ref=sc2_send.at[n], dst_ref=sc2_recv.at[n, at],
-            send_sem=s2s_sem.at[n, peer], recv_sem=s2r_sem.at[n, at],
-            device_id={"freq": peer}, device_id_type=MESH)
+            src_ref=sc2_send.at[n], dst_ref=sc2_recv.at[n, d],
+            send_sem=s2s_sem.at[n], recv_sem=s2r_sem.at[n],
+            device_id=plane_peer(d), device_id_type=MESH)
+
+    def collect(send, recv, ssem, rsem, n):
+        rest = recv.at[n, pl.ds(1, recv.shape[1] - 1)]
+        pltpu.make_async_remote_copy(
+            src_ref=rest, dst_ref=rest, send_sem=ssem.at[n], recv_sem=rsem.at[n],
+            device_id={"tile": lax.rem(me + 1, NTILE)}, device_id_type=MESH).wait()
+        recv[n, 0] = send[n]
+        return jnp.sum(recv[n], axis=0)
 
     def sum_start(n, gn, im):
         row = lax.broadcasted_iota(jnp.int32, (8, 128), 0)
         inn = sum(jnp.sum(i * i, axis=0, keepdims=True) for i in im)
         sc_send[n] = jnp.where(row == 0, gn, jnp.where(row == 1, inn, 0.0))
-
-        @pl.loop(1, NTILE)
-        def _(d):
+        for d in range(1, 8):
             scopy(n, d).start()
 
     def sum_middle(n):
-        rest = sc_recv.at[n, pl.ds(1, NTILE - 1)]
-        pltpu.make_async_remote_copy(
-            src_ref=rest, dst_ref=rest, send_sem=ss_sem.at[n], recv_sem=sr_sem.at[n],
-            device_id={"tile": lax.rem(me + 1, NTILE)}, device_id_type=MESH).wait()
-        sc_recv[n, 0] = sc_send[n]
-        part = jnp.sum(sc_recv[n], axis=0)
-        sc2_send[n] = part
-        for d in range(1, NF):
-            s2copy(n, lax.rem(fme + d, NF), fme).start()
+        sc2_send[n] = collect(sc_send, sc_recv, ss_sem, sr_sem, n)
+        for d in range(1, NPLANE):
+            s2copy(n, d).start()
 
     def sum_end(n):
-        for d in range(1, NF):
-            peer = lax.rem(fme + d, NF)
-            s2copy(n, peer, peer).wait()
-        sc2_recv[n, fme] = sc2_send[n]
-        both = jnp.sum(jnp.sum(sc2_recv[n], axis=0), axis=1, keepdims=True)
+        both = jnp.sum(collect(sc2_send, sc2_recv, s2s_sem, s2r_sem, n), axis=1, keepdims=True)
         return both[0:1] / both[1:2]
 
     def setup_gram():
@@ -307,14 +325,11 @@
 
     def mix(e, h, spec):
         swapped = [swap(s) for s in spec]
-        total = jnp.zeros((1, 128), F32)
         for fo in range(NF):
             o = jnp.zeros((32, 128), F32)
             for fi in range(NF):
                 o += gmap[fo, fi, 0] * spec[fi] + gmap[fo, fi, 1] * swapped[fi]
             fsend[e, h, pl.ds(fo * 32, 32), :] = o
-            total += jnp.sum(spec[fo] * o, axis=0, keepdims=True)
-        gn_ref[h] = total
 
     def read_spec(ref):
         return [ref[pl.ds(f * 32, 32), :] for f in range(NF)]
@@ -337,7 +352,7 @@
             fsend[0, 0, rows, :] = jnp.where(quarter, re, pltpu.roll(im, 32, 1))
             fsend[0, 1, rows, :] = jnp.where(quarter, pltpu.roll(re, 96, 1), im)
 
-    pl.semaphore_wait(bar, NTILE - 1 + NF - 1)
+    pl.semaphore_wait(bar, NTILE - 1 + met)
     fstart(0, 0)
     fstart(0, 1)
 
@@ -366,31 +381,34 @@
     setup_wide(vt, vn)
     setup_gram()
 
-    def adjoint_and_back(e, use, alpha):
+    def adjoint_and_back(e, use, between):
         k = NG // STEP - 1
         fsend[e, 0] = gather_products(e, 0, vn)
         fstart(e, 0)
         for i in range(k):
             gather_part(e, 1, vn, i)
-        a = alpha()
         fwait(e, 0)
-        use(0, a)
+        use(0)
         fstart(e + 1, 0)
         gather_part(e, 1, vn, k)
         fsend[e, 1] = pack(acc[...])
         fstart(e, 1)
+        between()
         fwait(e + 1, 0)
-        send_products(e + 1, 0, vt, frecv[e + 1, 0])
+        right[...] = rhs(frecv[e + 1, 0], 1.0)
+        for i in range(k):
+            send_part(e + 1, 0, vt, i)
         fwait(e, 1)
-        use(1, a)
+        use(1)
         fstart(e + 1, 1)
+        send_part(e + 1, 0, vt, k)
         fwait(e + 1, 1)
         send_products(e + 1, 1, vt, frecv[e + 1, 1])
-        return a
-
-    def first_use(h, a):
+
+    def first_use(h):
         spec0[h] = frecv[1, h]
         mix(2, h, read_spec(spec0.at[h]))
+        gn_ref[h] = jnp.sum(spec0[h] * fsend[2, h], axis=0, keepdims=True)
 
     adjoint_and_back(1, first_use, lambda: None)
 
@@ -399,20 +417,17 @@
     im_ref[1] = gather_products(2, 1, un)
     sum_start(0, gn_ref[0] + gn_ref[1], (im_ref[0], im_ref[1]))
     send_products(3, 1, ut, im_ref[1])
-    sum_middle(0)
-
-    def second_use(h, a):
-        comb_ref[h] = spec0[h] - a * frecv[3, h]
-        mix(4, h, read_spec(comb_ref.at[h]))
-
-    alpha0 = adjoint_and_back(3, second_use, lambda: sum_end(0))
-
+
+    adjoint_and_back(3, lambda h: mix(4, h, read_spec(frecv.at[3, h])), lambda: sum_middle(0))
+    alpha0 = sum_end(0)
     for h in range(2):
+        s1 = spec0[h] - alpha0 * frecv[3, h]
+        gn_ref[h] = jnp.sum(s1 * (fsend[2, h] - alpha0 * fsend[4, h]), axis=0, keepdims=True)
+        comb_ref[h] = s1
         r0_ref[h] = r0_ref[h] - alpha0 * im_ref[h]
 
-    @pl.loop(0, 2)
-    def _(h):
-        im_ref[h] = gather_products(4, h, un)
+    for h in range(2):
+        im_ref[h] = im_ref[h] - alpha0 * gather_products(4, h, un)
 
     sum_start(1, gn_ref[0] + gn_ref[1], (im_ref[0], im_ref[1]))
 
@@ -477,7 +492,7 @@
         out_specs=(hbm, hbm),
         scratch_shapes=[
             pltpu.VMEM((2, 2, 256, NTILE * 64), F32),
-            pltpu.VMEM((2, 2, NTILE * 64, 128), F32),
+            pltpu.VMEM((2, 2, 2, NTILE * 64, 128), F32),
             pltpu.VMEM((2, NG, 512, 512), BF16),
             pltpu.SMEM((2, NTILE), jnp.int32),
             dma((4,)), dma((2, NG)),
@@ -510,11 +525,11 @@
             pltpu.VMEM(pairs, F32),
             pltpu.VMEM((2, 1, 128), F32),
             pltpu.VMEM((2, 8, 128), F32),
-            pltpu.VMEM((2, NTILE, 8, 128), F32),
+            pltpu.VMEM((2, 8, 8, 128), F32),
             pltpu.VMEM((2, 8, 128), F32),
-            pltpu.VMEM((2, NF, 8, 128), F32),
+            pltpu.VMEM((2, NPLANE, 8, 128), F32),
             dma((3,)), dma((5, 2)), dma((5, 2, NG // STEP)), dma((5, 2, NF)), dma((5, 2, NF)),
-            dma((2,)), dma((2,)), dma((2, NF)), dma((2, NF)),
+            dma((2,)), dma((2,)), dma((2,)), dma((2,)),
         ],
         compiler_params=pltpu.CompilerParams(collective_id=0, has_side_effects=True, vmem_limit_bytes=ROOM),
         name="descent",

time: 131 us -> 127 us (0.969)
  Pallas kernels: 130 us -> 125 us
    pallas_call x1, Pallas kernels: 12 us -> 9.29 us  [body(): pl.pallas_call(setup_kernel, out_shape=(tiles, tiles), in_specs=[smem, hb...]
    pallas_call x1, Pallas kernels: 113 us -> 111 us  [body(): pl.pallas_call(main_kernel, out_shape=(jax.ShapeDtypeStruct(pairs, F32),...]
where the time goes in v4:
time: 127 us; the launch traced here: 126 us
  Pallas kernels  125 us (98%)
    pallas_call x1, Pallas kernels, body(): pl.pallas_call(main_kernel, out_shape=(jax.ShapeDtypeStruct(pairs, F32),...  111 us
    pallas_call x1, Pallas kernels, body(): pl.pallas_call(setup_kernel, out_shape=(tiles, tiles), in_specs=[smem, hb...  9.29 us
    pallas_call x1, Pallas kernels, body(): pl.pallas_call(update_kernel, grid=(32 // step,), out_shape=jax.ShapeDtyp...  4.49 us

profile of v4, /device:TPU:1, one launch (start us, length us, event | category | flops | bytes accessed | tf_op | source)
XLA Modules:
  0.0 126.5 jit_solution(801654300183372635)
XLA Ops:
  0.6 9.3 %setup.1 = (bf16[8,512,512]{2,1,0:T(8,128)(2,1)}, bf16[8,512,512]{2,1,0:T(8,128)(2,1)}) custom-call(s32[32,32]{1,0:T(8,128)} %bitcast.19, f32[2,256,2048]{2,1,0:T(8,128)} %bitcast.14, f32[2,256,2048]{2,1,0:T(8,128)} %bitcast.15), custom_call_target="tpu_custom_call" | custom-call | tf_op jit(solution)/shard_map/setup/pallas_call | solution.py:488
  9.9 111.4 %descent.1 = (f32[2,128,128]{2,1,0:T(8,128)}, f32[2,64,256]{2,1,0:T(8,128)}) custom-call(s32[64]{0:T(128)} %mute_ref.3, f32[4096,256]{1,0:T(8,128)} %bitcast.12, bf16[8,512,512]{2,1,0:T(8,128)(2,1)} %get-tuple-element.6.vt_hbm, bf16[8,512,512]{2,1,0:T(8,128)(2,1)} %get-tuple-element.7.ut_hbm, f32[2,64,256]{2,1,0:T(8,128)} %bitcast.17, ...), custom_call_target="tpu_custom_call" | custom-call | tf_op jit(solution)/shard_map/descent/pallas_call | solution.py:504
  121.3 0.0 copy-start
  121.3 4.5 %update.1 = f32[2,32,64,256]{3,2,1,0:T(8,128)} custom-call(s32[64]{0:T(128)} %mute_ref.3, f32[2,128,128]{2,1,0:T(8,128)} %get-tuple-element.8.comb_ref, bf16[32,256]{1,0:T(8,128)(2,1)} %constant.19.b3_ref, f32[2,32,64,256]{3,2,1,0:T(8,128)} %bitcast.13), custom_call_target="tpu_custom_call" | custom-call | tf_op jit(solution)/shard_map/update/pallas_call | solution.py:538
  125.8 0.0 copy-done
  125.8 0.7 copy.11
Async XLA Ops:
  121.3 4.5 %copy-start = (f32[2,64,256]{2,1,0:T(8,128)S(1)}, f32[2,64,256]{2,1,0:T(8,128)}, u32[]{:S(2)}) copy-start(f32[2,64,256]{2,1,0:T(8,128)} %get-tuple-element.9) | copy-start | bytes 393220
